TPU v7x, 32 devices: a whole 2x2x4 slice. The times are simulated.
32 devices in a mesh: chan: 8 (over z, y), win: 4 (over x, core).
Axes of the slice: x: 2, y: 2, z: 4, core: 2. Of those that a mesh axis runs over, the one named last changes fastest.
Arguments:
- spectra: bfloat16 [384, 16, 2, 1024], P('chan', 'win'), may hold values from -120 to 120
- sources: int32 [4], replicated, may hold values from 0 to 383
- bin_rows: int32 [4, 8, 32, 3], P(None, 'chan'), may hold values from -1 to 47, as said below
Outputs:
- stacked: float32 [4, 32, 4096], P(None, 'chan', 'win')
Inputs may be any that keep to these rules, and one draw needn't show every extreme that they name: `bin_rows`: for every step and every index d of chan, the entries name each of that device's 48 local receiver rows exactly once; within a bin the used slots come first and the rest are -1. In each step one bin uses all 3 slots on every device.
All inputs are finite; a program needn't handle non-finite values.
Results may differ from a plain program's by a relative error of at most 0.0099.
Values may be sent and summed in bfloat16 or wider, within the bound.
A program may use at most 768 MiB of HBM per device.

v0:
```python
import jax
import jax.numpy as jnp
from jax import lax
from jax.sharding import PartitionSpec as P

F = 1024
F0 = 32
NFFT = 8192
LMAX = 2048
HW = 32
NBINS = 32
MOST = 3
LAGS = 4096


epsilon_amp = 1e-06
phase_floor = 0.1


def broadcast(block, axis, source):
    block = jnp.where(lax.axis_index(axis) == source, block, jnp.zeros_like(block))
    return lax.psum(block, axis)


def band_matrix():
    index = jnp.arange(F, dtype=jnp.int32)
    inside = jnp.abs(index[:, None] - index[None, :]) <= HW
    return inside.astype(jnp.float32) / (2 * HW + 1)


def whiten(spectra):
    real_part = spectra[:, :, 0, :].astype(jnp.float32)
    imag_part = spectra[:, :, 1, :].astype(jnp.float32)
    amplitude = jnp.sqrt(real_part * real_part + imag_part * imag_part)
    smooth = jnp.dot(amplitude.reshape(-1, F), band_matrix(), precision=lax.Precision.HIGHEST)
    smooth = smooth.reshape(amplitude.shape) + epsilon_amp
    return jnp.stack([real_part / smooth, imag_part / smooth], axis=2).astype(jnp.bfloat16)


def cross_spectra(white, source):
    white_real = white[..., 0, :].astype(jnp.float32)
    white_imag = white[..., 1, :].astype(jnp.float32)
    source_real = source[..., 0, :].astype(jnp.float32)
    source_imag = source[..., 1, :].astype(jnp.float32)
    cross_real = white_real * source_real + white_imag * source_imag
    cross_imag = white_imag * source_real - white_real * source_imag
    return jnp.concatenate([cross_real, cross_imag], axis=-1).astype(jnp.bfloat16)


def lag_table(first_lag, lag_count):
    frequency = F0 + jnp.arange(F, dtype=jnp.int32)
    lag_index = first_lag + jnp.arange(lag_count, dtype=jnp.int32) - LMAX
    turn_count = jnp.mod(frequency[:, None] * lag_index[None, :], NFFT)
    angle_rad = turn_count.astype(jnp.float32) * (2.0 * jnp.pi / NFFT)
    cosine = jnp.cos(angle_rad)
    sine_part = jnp.sin(angle_rad)
    upper_half = jnp.concatenate([cosine, sine_part], axis=1)
    lower_half = jnp.concatenate([-sine_part, cosine], axis=1)
    return jnp.concatenate([upper_half, lower_half], axis=0).astype(jnp.bfloat16)


def correlate_block(cross_rows, first_lag, lag_count, windows):
    analytic = jnp.dot(
        cross_rows, lag_table(first_lag, lag_count), preferred_element_type=jnp.float32
    )
    analytic = analytic * (1.0 / jnp.sqrt(jnp.float32(F)))
    real_part = analytic[:, :lag_count]
    imag_part = analytic[:, lag_count:]
    magnitude = jnp.maximum(jnp.sqrt(real_part * real_part + imag_part * imag_part), phase_floor)
    terms = jnp.stack([real_part, real_part / magnitude, imag_part / magnitude], axis=1)
    return terms.reshape(-1, windows, 3, lag_count).sum(axis=1)


def weigh_stack(totals, counts, windows):
    traces = jnp.maximum(counts, 1.0) * windows
    linear = totals[..., 0, :]
    power = totals[..., 1, :] * totals[..., 1, :] + totals[..., 2, :] * totals[..., 2, :]
    return linear / jnp.sqrt(traces)[..., None] * power / traces[..., None]


def gather_rows(partial_value, slot_rows, chan_count):
    is_live = slot_rows >= 0
    safe_rows = jnp.maximum(slot_rows, 0)
    picked = jax.vmap(lambda block_rows, chosen: block_rows[chosen])(partial_value, safe_rows)
    picked = picked * is_live[..., None, None].astype(jnp.float32)
    step_count = slot_rows.shape[0]
    slot_count = NBINS * MOST // chan_count
    buffer = picked.reshape(step_count, chan_count, slot_count, 3, partial_value.shape[-1])
    live_mask = is_live.astype(jnp.float32).reshape(step_count, chan_count, slot_count)
    return (buffer, live_mask)


def fold_slots(received, live_mask):
    step_count, chan_count, slot_count = live_mask.shape
    bin_count = slot_count // MOST
    totals = received.reshape(step_count, chan_count, bin_count, MOST, 3, received.shape[-1]).sum(
        axis=(1, 3)
    )
    counts = live_mask.reshape(step_count, chan_count, bin_count, MOST).sum(axis=(1, 3))
    return (totals, counts)


def shards(spectra, sources, bin_rows):
    chan_dev = spectra.shape[0]
    win_dev = spectra.shape[1]
    chan_count = lax.axis_size("chan")
    windows = win_dev * lax.axis_size("win")
    step_count = sources.shape[0]
    white = whiten(spectra)
    owners = sources // chan_dev
    local_rows = sources % chan_dev
    gathered = []
    for step_index in range(step_count):
        own_row = lax.dynamic_index_in_dim(white, local_rows[step_index], 0, keepdims=False)
        gathered.append(broadcast(own_row, "chan", owners[step_index]))
    source = jnp.stack(gathered)
    cross_rows = cross_spectra(white[None], source[:, None]).reshape(-1, 2 * F)
    block_len = min(256, LAGS)
    block_count = LAGS // block_len

    def one_block(block):
        return correlate_block(cross_rows, block * block_len, block_len, win_dev)

    pieces = lax.map(one_block, jnp.arange(block_count, dtype=jnp.int32))
    pieces = pieces.reshape(block_count, step_count, chan_dev, 3, block_len)
    partial_value = jnp.transpose(pieces, (1, 2, 3, 0, 4)).reshape(step_count, chan_dev, 3, LAGS)
    slot_rows = bin_rows[:, 0]
    buffer, live_mask = gather_rows(partial_value, slot_rows, chan_count)
    received, live_got = (
        lax.all_to_all(buffer, "chan", split_axis=1, concat_axis=1, tiled=True),
        lax.all_to_all(live_mask, "chan", split_axis=1, concat_axis=1, tiled=True),
    )
    totals, counts = fold_slots(received, live_got)
    totals = lax.psum_scatter(totals, "win", scatter_dimension=3, tiled=True)
    return weigh_stack(totals, counts, windows)


def solution(mesh):
    in_specs = (P("chan", "win", None, None), P(), P(None, "chan", None, None))
    out_specs = P(None, "chan", "win")
    return jax.shard_map(shards, mesh=mesh, in_specs=in_specs, out_specs=out_specs, check_vma=False)
```

profile of v0, /device:TPU:0, one launch (start us, length us, event | category | flops | bytes accessed | tf_op | source)
XLA Modules:
  0.0 952.8 jit_solution(17982819426027233822)
XLA Ops:
  29.9 69.7 %all-reduce.3.cloned.1.call-done = (bf16[1,4,2,1024]{3,0,1,2:T(2,128)(2,1)}, bf16[1,4,2,1024]{3,0,1,2:T(2,128)(2,1)}, bf16[1,4,2,1024]{3,0,1,2:T(2,128)(2,1)}, bf16[1,4,2,1024]{3,0,1,2:T(2,128)(2,1)}) async-done(((bf16[1,4,2,1024]{3,0,1,2:T(2,128)(2,1)}, bf16[1,4,2,1024]{3,0,1,2:T(2,128)(2,1)}, bf16[1,4,2,1024]{3,0,1,2:T(2,128)(2,1)}, bf16[1,4,2,1024]{3,0,1,2:T(2,128)(2,1)}), ...) | async-done | bytes 65552 | tf_op jit(solution)/shard_map/psum | solution.py:22
  110.7 226.3 %while.12 = (s32[]{:T(128)}, f32[16,192,3,256]{3,1,2,0:T(8,128)}, s32[16]{0:T(128)S(1)}, bf16[768,2048]{1,0:T(8,128)(2,1)}, s32[]{:T(128)}, /*index=5*/s32[1]{0:T(128)}) while((s32[]{:T(128)}, f32[16,192,3,256]{3,1,2,0:T(8,128)}, s32[16]{0:T(128)S(1)}, bf16[768,2048]{1,0:T(8,128)(2,1)}, s32[]{:T(128)}, /*index=5*/s32[1]{0:T(128)}) %tuple.55), condition=%wide.region_6.7_spmd, body=%wide.region_4.6_spmd.sunk | while | flops 1626916352 | bytes 25373280 | solution.py:124
  111.9 4.7 fusion.55
  140.2 4.7 fusion.55
  168.5 4.7 fusion.55
  182.6 4.7 fusion.55
  196.7 4.7 fusion.55
  210.8 4.7 fusion.55
  239.1 4.7 fusion.55
  253.2 4.7 fusion.55
  337.0 13.8 %copy.118 = f32[16,4,48,3,256]{4,0,2,3,1:T(8,128)} copy(f32[16,4,48,3,256]{4,2,1,3,0:T(8,128)} %bitcast.99) | data formatting | bytes 18874368 | tf_op jit(solution)/shard_map/reshape | solution.py:125
  350.8 11.3 %reshape.190 = f32[4,48,3,4096]{3,1,2,0:T(8,128)} reshape(f32[4,48,3,16,256]{4,3,1,2,0:T(8,128)} %bitcast.96) | data formatting | bytes 18874368 | tf_op jit(solution)/shard_map/reshape | solution.py:126
  362.1 14.8 %copy.82 = f32[4,48,3,4096]{3,2,1,0:T(4,128)} copy(f32[4,48,3,4096]{3,1,2,0:T(8,128)} %reshape.190) | data formatting | bytes 18874368 | tf_op jit(solution)/shard_map/reshape | solution.py:126
  376.9 31.5 %gather_fusion = f32[384,3,4096]{2,1,0:T(4,128)} fusion(f32[4,48,3,4096]{3,2,1,0:T(4,128)} %copy.82, s32[384]{0:T(512)S(1)} %reshape.200), kind=kCustom, calls=%fused_computation | custom fusion | bytes 37751808 | tf_op jit(solution)/shard_map/vmap()/gather | solution.py:84
  408.4 12.3 %copy_multiply_fusion = f32[4,8,12,3,4096]{4,2,1,0,3:T(8,128)S(1)} fusion(f32[4,8,12,3,4096]{4,3,2,1,0:T(4,128)} %bitcast.94, f32[4,8,12]{2,1,0:T(8,128)S(1)} %reshape.199), kind=kLoop, calls=%fused_computation.30 | loop fusion | flops 4718592 | bytes 37750272 | tf_op jit(solution)/shard_map/mul | solution.py:85
  420.7 17.2 %copy.85 = f32[4,8,12,3,4096]{4,0,3,2,1:T(4,128)} copy(f32[4,8,12,3,4096]{4,2,1,0,3:T(8,128)S(1)} %copy_multiply_fusion) | data formatting | bytes 37748736 | tf_op jit(solution)/shard_map/mul | solution.py:85
  437.9 414.2 %all_to_all.10 = f32[4,8,12,3,4096]{4,0,3,2,1:T(4,128)} all-to-all(f32[4,8,12,3,4096]{4,0,3,2,1:T(4,128)} %copy.85), channel_id=1, replica_groups=mesh['chan'=8,'win'=4] {'chan'}, dimensions={1} | all-to-all | bytes 37748736 | tf_op jit(solution)/shard_map/all_to_all | solution.py:130
  852.2 10.9 %reduce_sum.44 = f32[4,12,3,4096]{3,0,2,1:T(4,128)S(1)} reduce(f32[4,8,12,3,4096]{4,0,3,2,1:T(4,128)} %all_to_all.10, f32[]{:T(128)} %constant.115.clone.1), dimensions={1}, to_apply=%region_7.8 | reduce | flops 4128768 | bytes 21233668 | tf_op jit(solution)/shard_map/reduce_sum | solution.py:96
  863.9 16.9 %copy.91 = f32[4,4,3,4096]{1,0,2,3:T(4,128)} copy(f32[4,4,3,4096]{3,0,2,1:T(4,128)S(1)} %reduce_sum.46) | data formatting | bytes 1572864
  880.9 18.1 %reshape.213 = f32[4096,48]{1,0:T(8,128)} reshape(f32[4096,3,4,4]{3,2,1,0:T(4,128)} %bitcast.95) | data formatting | bytes 1572864
  899.0 10.2 %all_to_all.11 = f32[4,8,12]{2,0,1:T(4,128)S(1)} all-to-all(f32[4,8,12]{2,0,1:T(4,128)S(1)} %copy.89), channel_id=1, replica_groups=mesh['chan'=8,'win'=4] {'chan'}, dimensions={1} | all-to-all | bytes 3072 | tf_op jit(solution)/shard_map/all_to_all | solution.py:131
  909.4 20.1 %reduce-scatter.4.cloned.1.call-done = f32[1024,48]{1,0:T(8,128)} async-done(((f32[4096,48]{1,0:T(8,128)}), f32[1024,48]{1,0:T(8,128)}) %reduce-scatter.4.cloned.1.call-update) | async-done | bytes 196624
  929.5 5.5 reshape.214
  935.1 5.3 fusion.44
  (257 shorter events, 207.3 us)
Async XLA Ops:
  6.5 93.1 %all-reduce.3.cloned.1.call-start = ((), (), s32[]{:S(2)}) async-start(), calls=%async_computation.4 | async-start | bytes 262144 | tf_op jit(solution)/shard_map/psum | solution.py:22
  21.3 5.7 copy-start.1
  26.3 903.2 %reduce-scatter.4.cloned.1.call-start = ((), (), s32[]{:S(2)}) async-start(), calls=%async_computation.3 | async-start | bytes 2621440
  105.4 1.9 copy-start
Sparse Core Ops, SparseCore 0:
  26.5 73.1 all-reduce.2
  899.1 30.3 reduce-scatter.3
where the time goes:
time: 960 us; the launch traced here: 953 us
  blocking collectives  424 us (44%)
  local copies, waits for them, and re-layouts  197 us (21%)
  other arithmetic  142 us (15%)
  waiting for transfers between devices  89.9 us (9%)
  matrix products  63.9 us (7%)
  between operations  23.8 us (2%)
  loops' own time  12 us (1%)
    all_to_all x1, blocking collectives, shards(): lax.all_to_all(buffer, 'chan', split_axis=1, concat_axis=1, tiled=True)  414 us
    another operation x17, other arithmetic  78.3 us
    psum x1, waiting for transfers between devices, broadcast(): return lax.psum(block, axis)  69.7 us
    dot_general x16, matrix products, correlate_block(): jnp.dot(cross_rows, lag_table(first_lag, lag_count), preferred_element_ty...  59.6 us
    unnamed x10, local copies, waits for them, and re-layouts  45.2 us
    gather x3, local copies, waits for them, and re-layouts, gather_rows(): block_rows[chosen]  31.8 us
    reduce_sum x16, other arithmetic, correlate_block(): return terms.reshape(-1, windows, 3, lag_count).sum(axis=1)  26.3 us
    reshape x2, local copies, waits for them, and re-layouts, shards(): jnp.transpose(pieces, (1, 2, 3, 0, 4))  26.1 us
  transfers between devices with their start and end apart: 2, of which 2 were waited for; matrix products, arithmetic and copies ran while one was open for 0% of the time, Pallas kernels for 0%

commit v1 on v0

v1 whole, which is shorter than its diff:
```python
import functools

import jax
import jax.numpy as jnp
import ml_dtypes
import numpy as np
from jax import lax
from jax.experimental import pallas as pl
from jax.experimental.pallas import tpu as pltpu
from jax.sharding import PartitionSpec as P

F = 1024
F0 = 32
NFFT = 8192
LMAX = 2048
HW = 32
NBINS = 32
MOST = 3
LAGS = 4096
CHUNK = 256

epsilon_amp = 1e-06
phase_floor = 0.1

f32 = jnp.float32
bf16 = jnp.bfloat16
MESH = pl.DeviceIdType.MESH


def lag_tables(lag_dev):
    blocks = LMAX // lag_dev
    units = lag_dev // CHUNK
    freq = F0 + np.arange(F, dtype=np.int64)

    def trig(lags):
        turn = (freq[:, None] * lags[None, :]) % NFFT
        angle = turn * (2.0 * np.pi / NFFT)
        scale = F ** -0.5
        return np.cos(angle).astype(ml_dtypes.bfloat16), np.sin(angle).astype(ml_dtypes.bfloat16), scale

    table = np.zeros((units, blocks, F, 2 * CHUNK), ml_dtypes.bfloat16)
    for u in range(units):
        for m in range(blocks):
            cosine, sine, scale = trig(m * lag_dev + u * CHUNK + np.arange(CHUNK))
            both = np.concatenate([cosine, sine], axis=1).astype(np.float32) * scale
            table[u, m] = both.astype(ml_dtypes.bfloat16)
    edge = np.zeros((F, 256), np.float32)
    cosine, sine, scale = trig((np.arange(blocks) + 1) * lag_dev)
    edge[:, :blocks] = cosine.astype(np.float32) * scale
    edge[:, 128 : 128 + blocks] = sine.astype(np.float32) * scale
    return table, edge.astype(ml_dtypes.bfloat16)


def dot(a, b):
    return jnp.dot(a, b, preferred_element_type=f32)


def smooth_band(amp, band):
    hi = amp.astype(bf16)
    lo = (amp - hi.astype(f32)).astype(bf16)
    count = F // 256
    parts = []
    for j in range(count):
        first, last = max(j - 1, 0), min(j + 2, count)
        piece = band[(first - j + 1) * 256 : (last - j + 1) * 256, :]
        cols = slice(first * 256, last * 256)
        parts.append(dot(hi[:, cols], piece) + dot(lo[:, cols], piece))
    return jnp.concatenate(parts, axis=1) * (1.0 / (2 * HW + 1)) + epsilon_amp


def whiten(re, im, band):
    inv = 1.0 / smooth_band(jnp.sqrt(re * re + im * im), band)
    return (re * inv).astype(bf16), (im * inv).astype(bf16)


def kernel(
    cfg,
    x_ref, srccol_ref, kcol_ref, cnt_ref, edge_ref, tab_hbm,
    o_ref,
    tab, sbuf, rsr, ag, wr_s, wi_s, sr_s, si_s, xs, wmat, ts, oe, traces,
    p1, r1, a2, b2, r2, a3, b3, r3, a4, b4, r4,
    tab_sem, rs_s, rs_r, ag_s, ag_r, s1, q1, s2, q2, s3, q3, s4, q4,
):
    nchan, nwin, steps, wd, chd, units, blocks = cfg
    g2, g4 = nwin // 2, nchan // 2
    rows = wd * chd
    me_c, me_w = lax.axis_index("chan"), lax.axis_index("win")
    w1, w2 = lax.rem(me_w, 2), me_w // 2
    c1, c2 = lax.rem(me_c, 2), me_c // 2

    def chan_dev(k):
        return (lax.rem(me_c + k, nchan), me_w)

    def dev1():
        return (me_c, me_w + 1 - 2 * w1)

    def dev2(k):
        return (me_c, lax.rem(w2 + k, g2) * 2 + w1)

    def dev3():
        return (me_c + 1 - 2 * c1, me_w)

    def dev4(k):
        return (lax.rem(c2 + k, g4) * 2 + c1, me_w)

    def table_copy(u):
        return pltpu.make_async_copy(tab_hbm.at[u], tab.at[u], tab_sem.at[u])

    def remote(src, dst, s, r, dev):
        return pltpu.make_async_remote_copy(
            src_ref=src, dst_ref=dst, send_sem=s, recv_sem=r, device_id=dev, device_id_type=MESH
        )

    for u in range(units):
        table_copy(u).start()

    barrier = pltpu.get_barrier_semaphore()
    partners = [chan_dev(k) for k in range(1, nchan)] + [dev1()] + [dev2(k) for k in range(1, g2)]
    for dev in partners:
        pl.semaphore_signal(barrier, inc=1, device_id=dev, device_id_type=MESH)

    piece = 2 * F // nchan
    col = lax.broadcasted_iota(jnp.int32, (steps * wd, rows), 1)
    pick = jnp.where(col == srccol_ref[...], 1.0, 0.0).astype(bf16)
    both = jnp.concatenate([dot(pick, x_ref[0]), dot(pick, x_ref[1])], axis=1).astype(bf16)
    for d in range(nchan):
        sbuf[d, :, :piece] = both[:, d * piece : (d + 1) * piece]
        sbuf[d, :, piece:] = cnt_ref[d]
    pl.semaphore_wait(barrier, len(partners))

    def rs_copy(k):
        return remote(
            sbuf.at[lax.rem(me_c + k, nchan)], rsr.at[k - 1], rs_s.at[k - 1], rs_r.at[k - 1], chan_dev(k)
        )

    def ag_copy(k):
        return remote(ag.at[me_c], ag.at[me_c], ag_s.at[k - 1], ag_r.at[k - 1], chan_dev(k))

    for k in range(1, nchan):
        rs_copy(k).start()

    kc = kcol_ref[...]
    wcol = lax.broadcasted_iota(jnp.int32, wmat.shape, 1)
    hit = (wcol == kc[:, 0:1]) | (wcol == kc[:, 1:2]) | (wcol == kc[:, 2:3])
    wmat[...] = jnp.where(hit, 1.0, 0.0).astype(bf16)
    bi = lax.broadcasted_iota(jnp.int32, (768, 256), 0)
    bj = lax.broadcasted_iota(jnp.int32, (768, 256), 1)
    band = jnp.where(jnp.abs(bi - 256 - bj) <= HW, 1.0, 0.0).astype(bf16)

    for k in range(1, nchan):
        rs_copy(k).wait()
    total = sbuf[me_c].astype(f32)
    for k in range(1, nchan):
        total = total + rsr[k - 1].astype(f32)
    ag[me_c] = total[:, :piece].astype(bf16)
    traces[...] = jnp.maximum(total[:, piece:], 1.0) * (wd * nwin)
    for k in range(1, nchan):
        ag_copy(k).start()

    wr, wi = whiten(x_ref[0].astype(f32), x_ref[1].astype(f32), band)
    wr_s[...] = wr
    wi_s[...] = wi

    for k in range(1, nchan):
        ag_copy(k).wait()
    half = nchan // 2
    sre = jnp.concatenate([ag[d] for d in range(half)], axis=1).astype(f32)
    sim = jnp.concatenate([ag[d] for d in range(half, nchan)], axis=1).astype(f32)
    sr, si = whiten(sre, sim, band)
    sr_s[...] = sr.astype(f32)
    si_s[...] = si.astype(f32)

    for w in range(wd):
        here = slice(w * chd, (w + 1) * chd)
        wrw = wr_s[here, :].astype(f32)
        wiw = wi_s[here, :].astype(f32)
        for s in range(steps):
            i = s * wd + w
            a, b = sr_s[i : i + 1, :], si_s[i : i + 1, :]
            xs[s, here, :] = (wrw * a + wiw * b).astype(bf16)
            xs[s, slice(rows + w * chd, rows + (w + 1) * chd), :] = (wiw * a - wrw * b).astype(bf16)

    def add_terms(sign, s, re, im, lanes):
        inv = lax.rsqrt(jnp.maximum(re * re + im * im, phase_floor * phase_floor))
        for q, value in enumerate((re, re * inv, im * inv)):
            total = value[:chd]
            for w in range(1, wd):
                total = total + value[w * chd : (w + 1) * chd]
            first = (s * 3 + q) * chd
            ts[sign, first : first + chd, :lanes] = total.astype(bf16)

    for s in range(steps):
        res = dot(xs[s], edge_ref[...])
        add_terms(1, s, res[:rows, :128] + res[rows:, 128:], res[rows:, :128] - res[:rows, 128:], 128)
    oe[...] = dot(wmat[...], ts[1, :, :128])

    def compute(u, m):
        for s in range(steps):
            res = dot(xs[s], tab[u, m])
            a, c = res[:rows, :CHUNK], res[:rows, CHUNK:]
            d, b = res[rows:, :CHUNK], res[rows:, CHUNK:]
            add_terms(0, s, a - b, c + d, CHUNK)
            add_terms(1, s, a + b, d - c, CHUNK)
        pos = blocks + m
        neg = blocks - 1 - m
        part = p1.shape[3:]
        p1[u, pos % 2, pos // 2] = dot(wmat[...], ts[0]).reshape(part)
        lane = lax.broadcasted_iota(jnp.int32, (wmat.shape[0], CHUNK), 1)
        value = dot(wmat[...], ts[1])
        value = jnp.where((lane + u) == 0, oe[:, m : m + 1], value)
        p1[u, neg % 2, neg // 2] = value.reshape(part)

    def copy1(u):
        return remote(p1.at[u, 1 - w1], r1.at[u], s1.at[u], q1.at[u], dev1())

    def copy2(u, k):
        return remote(
            b2.at[u, lax.rem(w2 + k, g2)], r2.at[u, k - 1], s2.at[u, k - 1], q2.at[u, k - 1], dev2(k)
        )

    def copy3(u):
        return remote(b3.at[u, 1 - c1], r3.at[u], s3.at[u], q3.at[u], dev3())

    def copy4(u, k):
        return remote(
            b4.at[u, lax.rem(c2 + k, g4)], r4.at[u, k - 1], s4.at[u, k - 1], q4.at[u, k - 1], dev4(k)
        )

    def stage2(u):
        copy1(u).wait()
        for i in range(g2):
            b2[u, i] = (p1[u, w1, i] + r1[u, i]).astype(bf16)
        for k in range(1, g2):
            copy2(u, k).start()
        a2[u] = p1[u, w1, w2] + r1[u, w2]

    def stage3(u):
        for k in range(1, g2):
            copy2(u, k).wait()
        for i in range(2):
            total = a2[u, i]
            for k in range(1, g2):
                total = total + r2[u, k - 1, i].astype(f32)
            a3[u, i] = total
            b3[u, i] = total.astype(bf16)
        copy3(u).start()

    def stage4(u):
        copy3(u).wait()
        for i in range(g4):
            total = a3[u, c1, i] + r3[u, i].astype(f32)
            a4[u, i] = total
            b4[u, i] = total.astype(bf16)
        for k in range(1, g4):
            copy4(u, k).start()

    def stage5(u):
        for k in range(1, g4):
            copy4(u, k).wait()
        total = a4[u, c2]
        for k in range(1, g4):
            total = total + r4[u, k - 1].astype(f32)
        n = total.shape[0] // 3
        lin, pr, pi = total[:n], total[n : 2 * n], total[2 * n :]
        count = traces[:n, 0:1]
        o_ref[u] = lin * lax.rsqrt(count) * ((pr * pr + pi * pi) / count)

    def turn(v, carry):
        @pl.when(v < units)
        def _():
            table_copy(v).wait()
            compute(v, 0)

        @pl.when((v >= 1) & (v < units + 1))
        def _():
            stage2(v - 1)

        @pl.when((v >= 2) & (v < units + 2))
        def _():
            stage3(v - 2)

        @pl.when((v >= 3) & (v < units + 3))
        def _():
            stage4(v - 3)

        @pl.when(v >= 4)
        def _():
            stage5(v - 4)

        @pl.when(v < units)
        def _():
            for m in range(1, blocks):
                compute(v, m)
            copy1(v).start()

        return carry

    lax.fori_loop(0, units + 4, turn, 0)


def shards(spectra, sources, bin_rows):
    chd, wd = spectra.shape[0], spectra.shape[1]
    steps = sources.shape[0]
    nchan, nwin = lax.axis_size("chan"), lax.axis_size("win")
    lag_dev = LAGS // nwin
    units, blocks = lag_dev // CHUNK, nwin // 2
    bl = NBINS // nchan
    rows = wd * chd
    g2, g4 = nwin // 2, nchan // 2
    me = lax.axis_index("chan")

    x = jnp.transpose(spectra, (2, 1, 0, 3)).reshape(2, rows, F)
    loc = sources - me * chd
    ok = (loc >= 0) & (loc < chd)
    srccol = jnp.where(ok[:, None], loc[:, None] + jnp.arange(wd, dtype=jnp.int32)[None] * chd, -1)
    srccol = srccol.reshape(steps * wd, 1)

    slots = bin_rows[:, 0].reshape(steps, g4, 2, bl, MOST)
    slots = jnp.transpose(slots, (2, 1, 0, 3, 4))[:, :, None]
    step_at = jnp.arange(steps, dtype=jnp.int32)[:, None, None] * (3 * chd)
    term_at = jnp.arange(3, dtype=jnp.int32)[:, None, None, None] * chd
    kcol = jnp.where(slots >= 0, slots + step_at + term_at, -1).reshape(NBINS * 3 * steps, MOST)
    live = jnp.sum((bin_rows[:, 0] >= 0).astype(f32), axis=-1).reshape(steps, nchan, bl)
    live = jnp.transpose(live, (1, 0, 2)).reshape(nchan, steps * bl, 1)
    live = jnp.pad(live, ((0, 0), (0, steps * wd - steps * bl), (0, 0)))
    cnt = jnp.broadcast_to(live, (nchan, steps * wd, 128)).astype(bf16)

    table, edge = lag_tables(lag_dev)
    per = NBINS * 3 * steps // nchan
    piece = 2 * F // nchan
    tail = (per, CHUNK)
    cfg = (nchan, nwin, steps, wd, chd, units, blocks)
    dma = pltpu.SemaphoreType.DMA
    vmem = pl.BlockSpec(memory_space=pltpu.VMEM)
    out = pl.pallas_call(
        functools.partial(kernel, cfg),
        out_shape=jax.ShapeDtypeStruct((units, steps * bl, CHUNK), f32),
        in_specs=[vmem] * 5 + [pl.BlockSpec(memory_space=pl.ANY)],
        out_specs=vmem,
        scratch_shapes=[
            pltpu.VMEM((units, blocks, F, 2 * CHUNK), bf16),
            pltpu.VMEM((nchan, steps * wd, piece + 128), bf16),
            pltpu.VMEM((nchan - 1, steps * wd, piece + 128), bf16),
            pltpu.VMEM((nchan, steps * wd, piece), bf16),
            pltpu.VMEM((rows, F), bf16),
            pltpu.VMEM((rows, F), bf16),
            pltpu.VMEM((steps * wd, F), f32),
            pltpu.VMEM((steps * wd, F), f32),
            pltpu.VMEM((steps, 2 * rows, F), bf16),
            pltpu.VMEM((NBINS * 3 * steps, 3 * steps * chd), bf16),
            pltpu.VMEM((2, 3 * steps * chd, CHUNK), bf16),
            pltpu.VMEM((NBINS * 3 * steps, 128), f32),
            pltpu.VMEM((steps * wd, 128), f32),
            pltpu.VMEM((units, 2, g2, 2, g4) + tail, f32),
            pltpu.VMEM((units, g2, 2, g4) + tail, f32),
            pltpu.VMEM((units, 2, g4) + tail, f32),
            pltpu.VMEM((units, g2, 2, g4) + tail, bf16),
            pltpu.VMEM((units, g2 - 1, 2, g4) + tail, bf16),
            pltpu.VMEM((units, 2, g4) + tail, f32),
            pltpu.VMEM((units, 2, g4) + tail, bf16),
            pltpu.VMEM((units, g4) + tail, bf16),
            pltpu.VMEM((units, g4) + tail, f32),
            pltpu.VMEM((units, g4) + tail, bf16),
            pltpu.VMEM((units, g4 - 1) + tail, bf16),
            dma((units,)),
            dma((nchan - 1,)), dma((nchan - 1,)), dma((nchan - 1,)), dma((nchan - 1,)),
            dma((units,)), dma((units,)),
            dma((units, g2 - 1)), dma((units, g2 - 1)),
            dma((units,)), dma((units,)),
            dma((units, g4 - 1)), dma((units, g4 - 1)),
        ],
        compiler_params=pltpu.CompilerParams(
            collective_id=0, has_side_effects=True, vmem_limit_bytes=56 * 1024 * 1024
        ),
        name="stack",
    )(x, srccol, kcol, cnt, jnp.asarray(edge), jnp.asarray(table))
    out = jnp.transpose(out, (1, 0, 2)).reshape(steps, bl, lag_dev)
    mirrored = jnp.roll(jnp.flip(out, axis=-1), 1, axis=-1)
    return jnp.where(lax.axis_index("win") < blocks, mirrored, out)


def solution(mesh):
    in_specs = (P("chan", "win", None, None), P(), P(None, "chan", None, None))
    out_specs = P(None, "chan", "win")
    return jax.shard_map(shards, mesh=mesh, in_specs=in_specs, out_specs=out_specs, check_vma=False)
```

time: 960 us -> 67.7 us (0.07)
  blocking collectives: 424 us -> 0 us
  local copies, waits for them, and re-layouts: 197 us -> 6.96 us
  other arithmetic: 142 us -> 3.84 us
  waiting for transfers between devices: 89.9 us -> 0 us
  matrix products: 63.9 us -> 0 us
  Pallas kernels: 0 us -> 56.5 us
  between operations: 23.8 us -> 0.09 us
  loops' own time: 12 us -> 0 us
    all_to_all x2 -> x0, blocking collectives: 424 us -> none  [the longest x1 414 us: shards(): lax.all_to_all(buffer, 'chan', split_axis=1, concat_axis=1, tiled=True)]
    another operation x17 -> x0, other arithmetic: 78.3 us -> none
    psum x1 -> x0, waiting for transfers between devices: 69.7 us -> none  [broadcast(): return lax.psum(block, axis)]
    dot_general x17 -> x0, matrix products: 63.9 us -> none  [the longest x16 59.6 us: correlate_block(): jnp.dot(cross_rows, lag_table(first_lag, lag_count), preferred_element_ty...]
    pallas_call x0 -> x1, Pallas kernels: none -> 56.5 us  [shards(): pl.pallas_call(functools.partial(kernel, cfg), out_shape=jax.ShapeDtypeSt...]
    unnamed x10 -> x2, local copies, waits for them, and re-layouts: 45.2 us -> 0.84 us
    reshape x3 -> x1, local copies, waits for them, and re-layouts: 39.9 us -> 0.05 us  [shards(): out = jnp.transpose(out, (1, 0, 2)).reshape(steps, bl, lag_dev)]
    reduce_sum x20 -> x1, other arithmetic: 38.2 us -> 0.72 us  [shards(): jnp.sum((bin_rows[:, 0] >= 0).astype(f32), axis=-1)]
  transfers between devices with their start and end apart: 2 -> 0, of which waited for: 2 -> 0; matrix products, arithmetic and copies ran while one was open for 0% -> 0% of each run, Pallas kernels for 0% -> 0%
where the time goes in v1:
time: 67.7 us; the launch traced here: 67.4 us
  Pallas kernels  56.5 us (83%)
  local copies, waits for them, and re-layouts  6.96 us (10%)
  other arithmetic  3.84 us (6%)
    pallas_call x1, Pallas kernels, shards(): pl.pallas_call(functools.partial(kernel, cfg), out_shape=jax.ShapeDtypeSt...  56.5 us
    transpose x1, local copies, waits for them, and re-layouts, shards(): x = jnp.transpose(spectra, (2, 1, 0, 3)).reshape(2, rows, F)  2.44 us

profile of v1, /device:TPU:0, one launch (start us, length us, event | category | flops | bytes accessed | tf_op | source)
XLA Modules:
  0.0 67.4 jit_solution(14266567096515032015)
XLA Ops:
  0.0 0.7 compare_and_fusion
  0.7 0.1 add_select_fusion.1
  0.7 0.7 %fusion = bf16[4,32]{1,0:T(4,128)(2,1)S(1)} fusion(s32[4,1,32,3]{2,1,3,0:T(1,128)} %param.7), kind=kLoop, calls=%fused_computation.5 | loop fusion | flops 1024 | bytes 1792 | tf_op jit(solution)/shard_map/reduce_sum | solution.py:323
  1.5 0.7 select_n.32.srccol_ref
  2.1 0.1 convert_element_type.15
  2.2 0.1 copy.15
  2.3 0.1 copy.16
  2.4 0.7 %reduce.1 = s32[4,32,3]{1,2,0:T(4,128)S(1)} reduce(s32[4,1,32,3]{2,1,3,0:T(1,128)} %param.7, s32[]{:T(128)} %constant.16.clone.1), dimensions={1}, to_apply=%param.7.reduce_sub_computation | reduce | bytes 3076 | tf_op args[2]
  3.1 0.7 %broadcast_in_dim.44.cnt_ref = bf16[8,16,128]{2,1,0:T(8,128)(2,1)} broadcast(bf16[8,16]{1,0:T(8,128)(2,1)S(1)} %copy.16), dimensions={0,1} | broadcast | bytes 33024 | tf_op jit(solution)/shard_map/broadcast_in_dim | solution.py:326
  3.8 0.1 reshape_squeeze.3
  4.0 0.3 copy.13
  4.3 0.1 add_bitcast_fusion
  4.4 0.3 copy.14
  4.8 0.1 add.61
  4.8 0.1 add.62
  5.0 0.8 %add_select_fusion.kcol_ref = s32[384,3]{1,0:T(8,128)} fusion(pred[384,3]{1,0:T(8,128)(4,1)S(1)} %bitcast.19, s32[384,3]{1,0:T(8,128)S(1)} %bitcast.16, s32[384]{0:T(512)S(1)} %add.62), kind=kLoop, calls=%fused_computation | loop fusion | flops 2304 | bytes 11904 | tf_op jit(solution)/shard_map/jit(_where)/select_n | solution.py:322
  5.8 2.4 %copy.12 = bf16[2,4,48,1024]{3,2,1,0:T(8,128)(2,1)} copy(bf16[2,4,48,1024]{3,0,1,2:T(2,128)(2,1)} %bitcast.15) | data formatting | bytes 1572864 | tf_op jit(solution)/shard_map/transpose | solution.py:312
  8.2 56.5 %stack.1 = f32[4,16,256]{2,1,0:T(8,128)} custom-call(bf16[2,192,1024]{2,1,0:T(8,128)(2,1)} %bitcast.14, s32[16,1]{1,0:T(8,128)} %select_n.32.srccol_ref, s32[384,3]{1,0:T(8,128)} %add_select_fusion.kcol_ref, bf16[8,16,128]{2,1,0:T(8,128)(2,1)} %broadcast_in_dim.44.cnt_ref, bf16[1024,256]{1,0:T(8,128)(2,1)} %constant.8.clone.edge_ref, ...), custom_call_target="tpu_custom_call" | custom-call | tf_op jit(solution)/shard_map/stack/pallas_call | solution.py:335
  64.7 0.9 %copy.18 = f32[16,4,256]{2,1,0:T(4,128)S(1)} copy(f32[16,4,256]{2,0,1:T(8,128)} %bitcast.17) | data formatting | bytes 131072 | tf_op jit(solution)/shard_map/transpose | solution.py:377
  65.7 0.1 slice.16
  65.8 0.7 %reverse.2 = f32[4,4,1024]{2,1,0:T(4,128)S(1)} reverse(f32[4,4,1024]{2,1,0:T(4,128)S(1)} %bitcast.18), dimensions={2} | reverse | bytes 131072
  66.5 0.1 slice.17
  66.6 0.7 %maximum_select_fusion = f32[4,4,1024]{2,1,0:T(4,128)} fusion(f32[4,4,1024]{2,1,0:T(4,128)S(1)} %reshape.81, f32[4,4,1023]{2,1,0:T(4,128)S(1)} %slice.17, f32[4,4,1]{2,1,0:T(4,128)S(1)} %slice.15, pred[]{:T(512)S(6)} %lt.6), kind=kLoop, calls=%fused_computation.2 | loop fusion | flops 32768 | bytes 196609 | tf_op jit(solution)/shard_map/jit(_where)/select_n | solution.py:379
  (8 shorter events, 0.2 us)

commit v2 on v1

--- a/solution.py
+++ b/solution.py
@@ -17,7 +17,7 @@
 NBINS = 32
 MOST = 3
 LAGS = 4096
-CHUNK = 256
+CHUNK = 128
 
 epsilon_amp = 1e-06
 phase_floor = 0.1
@@ -75,9 +75,9 @@
 
 def kernel(
     cfg,
-    x_ref, srccol_ref, kcol_ref, cnt_ref, edge_ref, tab_hbm,
+    x_ref, sources_ref, bins_ref, edge_ref, tab_hbm,
     o_ref,
-    tab, sbuf, rsr, ag, wr_s, wi_s, sr_s, si_s, xs, wmat, ts, oe, traces,
+    tab, sbuf, rsr, ag, wr_s, wi_s, sr_s, si_s, xs, wmat, ts, oe, traces, fin,
     p1, r1, a2, b2, r2, a3, b3, r3, a4, b4, r4,
     tab_sem, rs_s, rs_r, ag_s, ag_r, s1, q1, s2, q2, s3, q3, s4, q4,
 ):
@@ -120,12 +120,34 @@
         pl.semaphore_signal(barrier, inc=1, device_id=dev, device_id_type=MESH)
 
     piece = 2 * F // nchan
+    bl = NBINS // nchan
+    row = lax.broadcasted_iota(jnp.int32, (steps * wd, rows), 0)
     col = lax.broadcasted_iota(jnp.int32, (steps * wd, rows), 1)
-    pick = jnp.where(col == srccol_ref[...], 1.0, 0.0).astype(bf16)
+    want = jnp.full(row.shape, -1, jnp.int32)
+    for s in range(steps):
+        loc = sources_ref[s] - me_c * chd
+        loc = jnp.where((loc >= 0) & (loc < chd), loc, -wd * chd - 1)
+        want = jnp.where(row // wd == s, (row % wd) * chd + loc, want)
+    pick = jnp.where(col == want, 1.0, 0.0).astype(bf16)
     both = jnp.concatenate([dot(pick, x_ref[0]), dot(pick, x_ref[1])], axis=1).astype(bf16)
+    slots = bins_ref[...].reshape(steps * NBINS, MOST)
+    live = jnp.sum(jnp.where(slots >= 0, 1.0, 0.0), axis=1, keepdims=True)
+    live = jnp.broadcast_to(live, (steps * NBINS, 128)).astype(bf16)
+
+    def row_of(shape, dims):
+        i = lax.broadcasted_iota(jnp.int32, shape, len(shape) - 2)
+        b = sum(lax.broadcasted_iota(jnp.int32, shape, d) * size for d, size in dims)
+        here = (i // bl) * NBINS + b * bl + i % bl
+        hit = lax.broadcasted_iota(jnp.int32, shape, len(shape) - 1) == here
+        return jnp.where(hit, 1.0, 0.0), i // bl
+
+    shape = (nchan, steps * bl, steps * NBINS)
+    chosen, _ = row_of(shape, [(0, 1)])
+    cnt = dot(chosen.reshape(nchan * steps * bl, steps * NBINS).astype(bf16), live).astype(bf16)
     for d in range(nchan):
         sbuf[d, :, :piece] = both[:, d * piece : (d + 1) * piece]
-        sbuf[d, :, piece:] = cnt_ref[d]
+        sbuf[d, :, piece:] = jnp.zeros((steps * wd, 128), bf16)
+        sbuf[d, : steps * bl, piece:] = cnt[d * steps * bl : (d + 1) * steps * bl]
     pl.semaphore_wait(barrier, len(partners))
 
     def rs_copy(k):
@@ -139,13 +161,12 @@
     for k in range(1, nchan):
         rs_copy(k).start()
 
-    kc = kcol_ref[...]
-    wcol = lax.broadcasted_iota(jnp.int32, wmat.shape, 1)
-    hit = (wcol == kc[:, 0:1]) | (wcol == kc[:, 1:2]) | (wcol == kc[:, 2:3])
-    wmat[...] = jnp.where(hit, 1.0, 0.0).astype(bf16)
     bi = lax.broadcasted_iota(jnp.int32, (768, 256), 0)
     bj = lax.broadcasted_iota(jnp.int32, (768, 256), 1)
     band = jnp.where(jnp.abs(bi - 256 - bj) <= HW, 1.0, 0.0).astype(bf16)
+    wr, wi = whiten(x_ref[0].astype(f32), x_ref[1].astype(f32), band)
+    wr_s[...] = wr
+    wi_s[...] = wi
 
     for k in range(1, nchan):
         rs_copy(k).wait()
@@ -157,9 +178,18 @@
     for k in range(1, nchan):
         ag_copy(k).start()
 
-    wr, wi = whiten(x_ref[0].astype(f32), x_ref[1].astype(f32), band)
-    wr_s[...] = wr
-    wi_s[...] = wi
+    shape = (2, g4, 3, steps * bl, steps * NBINS)
+    chosen, step = row_of(shape, [(0, 1), (1, 2)])
+    chosen = chosen.reshape(-1, steps * NBINS).astype(bf16)
+    offset = (step * 3 + lax.broadcasted_iota(jnp.int32, shape, 2)).astype(f32) * chd
+    offset = offset.reshape(-1, steps * NBINS)[:, 0:1]
+    slots_at = dot(chosen, slots.astype(f32).astype(bf16))
+    slots_at = jnp.where(slots_at >= 0.0, slots_at + offset, -1.0)
+    wcol = lax.broadcasted_iota(jnp.int32, wmat.shape, 1).astype(f32)
+    hit = wcol == slots_at[:, 0:1]
+    for k in range(1, MOST):
+        hit = hit | (wcol == slots_at[:, k : k + 1])
+    wmat[...] = jnp.where(hit, 1.0, 0.0).astype(bf16)
 
     for k in range(1, nchan):
         ag_copy(k).wait()
@@ -180,35 +210,37 @@
             xs[s, here, :] = (wrw * a + wiw * b).astype(bf16)
             xs[s, slice(rows + w * chd, rows + (w + 1) * chd), :] = (wiw * a - wrw * b).astype(bf16)
 
-    def add_terms(sign, s, re, im, lanes):
+    def add_terms(sign, s, re, im):
         inv = lax.rsqrt(jnp.maximum(re * re + im * im, phase_floor * phase_floor))
         for q, value in enumerate((re, re * inv, im * inv)):
             total = value[:chd]
             for w in range(1, wd):
                 total = total + value[w * chd : (w + 1) * chd]
             first = (s * 3 + q) * chd
-            ts[sign, first : first + chd, :lanes] = total.astype(bf16)
+            ts[first : first + chd, sign * CHUNK : (sign + 1) * CHUNK] = total.astype(bf16)
 
     for s in range(steps):
         res = dot(xs[s], edge_ref[...])
-        add_terms(1, s, res[:rows, :128] + res[rows:, 128:], res[rows:, :128] - res[:rows, 128:], 128)
-    oe[...] = dot(wmat[...], ts[1, :, :128])
+        add_terms(1, s, res[:rows, :128] + res[rows:, 128:], res[rows:, :128] - res[:rows, 128:])
+    oe[...] = dot(wmat[...], ts[:, CHUNK:])
 
     def compute(u, m):
+        res = dot(xs[0], tab[u, m])
         for s in range(steps):
-            res = dot(xs[s], tab[u, m])
+            later = dot(xs[s + 1], tab[u, m]) if s + 1 < steps else None
             a, c = res[:rows, :CHUNK], res[:rows, CHUNK:]
             d, b = res[rows:, :CHUNK], res[rows:, CHUNK:]
-            add_terms(0, s, a - b, c + d, CHUNK)
-            add_terms(1, s, a + b, d - c, CHUNK)
+            add_terms(0, s, a - b, c + d)
+            add_terms(1, s, a + b, d - c)
+            res = later
         pos = blocks + m
         neg = blocks - 1 - m
         part = p1.shape[3:]
-        p1[u, pos % 2, pos // 2] = dot(wmat[...], ts[0]).reshape(part)
+        value = dot(wmat[...], ts[...])
+        p1[u, pos % 2, pos // 2] = value[:, :CHUNK].reshape(part).astype(bf16)
         lane = lax.broadcasted_iota(jnp.int32, (wmat.shape[0], CHUNK), 1)
-        value = dot(wmat[...], ts[1])
-        value = jnp.where((lane + u) == 0, oe[:, m : m + 1], value)
-        p1[u, neg % 2, neg // 2] = value.reshape(part)
+        mirror = jnp.where((lane + u) == 0, oe[:, m : m + 1], value[:, CHUNK:])
+        p1[u, neg % 2, neg // 2] = mirror.reshape(part).astype(bf16)
 
     def copy1(u):
         return remote(p1.at[u, 1 - w1], r1.at[u], s1.at[u], q1.at[u], dev1())
@@ -229,10 +261,10 @@
     def stage2(u):
         copy1(u).wait()
         for i in range(g2):
-            b2[u, i] = (p1[u, w1, i] + r1[u, i]).astype(bf16)
+            b2[u, i] = (p1[u, w1, i].astype(f32) + r1[u, i].astype(f32)).astype(bf16)
         for k in range(1, g2):
             copy2(u, k).start()
-        a2[u] = p1[u, w1, w2] + r1[u, w2]
+        a2[u] = p1[u, w1, w2].astype(f32) + r1[u, w2].astype(f32)
 
     def stage3(u):
         for k in range(1, g2):
@@ -262,8 +294,8 @@
             total = total + r4[u, k - 1].astype(f32)
         n = total.shape[0] // 3
         lin, pr, pi = total[:n], total[n : 2 * n], total[2 * n :]
-        count = traces[:n, 0:1]
-        o_ref[u] = lin * lax.rsqrt(count) * ((pr * pr + pi * pi) / count)
+        count = traces[:n, :]
+        fin[u] = lin * lax.rsqrt(count) * ((pr * pr + pi * pi) / count)
 
     def turn(v, carry):
         @pl.when(v < units)
@@ -296,6 +328,22 @@
         return carry
 
     lax.fori_loop(0, units + 4, turn, 0)
+
+    ri = lax.broadcasted_iota(jnp.int32, (CHUNK, CHUNK), 0)
+    rj = lax.broadcasted_iota(jnp.int32, (CHUNK, CHUNK), 1)
+    flip = jnp.where(ri + rj == CHUNK, 1.0, 0.0).astype(bf16)
+    lane = lax.broadcasted_iota(jnp.int32, fin.shape[1:], 1)
+    for u in range(units):
+        value = fin[units - 1 - u]
+        hi = value.astype(bf16)
+        rest = value - hi.astype(f32)
+        mid = rest.astype(bf16)
+        low = (rest - mid.astype(f32)).astype(bf16)
+        value = dot(hi, flip) + dot(mid, flip) + dot(low, flip)
+        value = jnp.where(lane == 0, fin[(units - u) % units], value)
+        value = jnp.where(lane * 0 + me_w < blocks, value, fin[u])
+        for s in range(steps):
+            o_ref[s, :, u * CHUNK : (u + 1) * CHUNK] = value[s * bl : (s + 1) * bl]
 
 
 def shards(spectra, sources, bin_rows):
@@ -307,23 +355,7 @@
     bl = NBINS // nchan
     rows = wd * chd
     g2, g4 = nwin // 2, nchan // 2
-    me = lax.axis_index("chan")
-
     x = jnp.transpose(spectra, (2, 1, 0, 3)).reshape(2, rows, F)
-    loc = sources - me * chd
-    ok = (loc >= 0) & (loc < chd)
-    srccol = jnp.where(ok[:, None], loc[:, None] + jnp.arange(wd, dtype=jnp.int32)[None] * chd, -1)
-    srccol = srccol.reshape(steps * wd, 1)
-
-    slots = bin_rows[:, 0].reshape(steps, g4, 2, bl, MOST)
-    slots = jnp.transpose(slots, (2, 1, 0, 3, 4))[:, :, None]
-    step_at = jnp.arange(steps, dtype=jnp.int32)[:, None, None] * (3 * chd)
-    term_at = jnp.arange(3, dtype=jnp.int32)[:, None, None, None] * chd
-    kcol = jnp.where(slots >= 0, slots + step_at + term_at, -1).reshape(NBINS * 3 * steps, MOST)
-    live = jnp.sum((bin_rows[:, 0] >= 0).astype(f32), axis=-1).reshape(steps, nchan, bl)
-    live = jnp.transpose(live, (1, 0, 2)).reshape(nchan, steps * bl, 1)
-    live = jnp.pad(live, ((0, 0), (0, steps * wd - steps * bl), (0, 0)))
-    cnt = jnp.broadcast_to(live, (nchan, steps * wd, 128)).astype(bf16)
 
     table, edge = lag_tables(lag_dev)
     per = NBINS * 3 * steps // nchan
@@ -332,10 +364,10 @@
     cfg = (nchan, nwin, steps, wd, chd, units, blocks)
     dma = pltpu.SemaphoreType.DMA
     vmem = pl.BlockSpec(memory_space=pltpu.VMEM)
-    out = pl.pallas_call(
+    return pl.pallas_call(
         functools.partial(kernel, cfg),
-        out_shape=jax.ShapeDtypeStruct((units, steps * bl, CHUNK), f32),
-        in_specs=[vmem] * 5 + [pl.BlockSpec(memory_space=pl.ANY)],
+        out_shape=jax.ShapeDtypeStruct((steps, bl, lag_dev), f32),
+        in_specs=[vmem, pl.BlockSpec(memory_space=pltpu.SMEM), vmem, vmem] + [pl.BlockSpec(memory_space=pl.ANY)],
         out_specs=vmem,
         scratch_shapes=[
             pltpu.VMEM((units, blocks, F, 2 * CHUNK), bf16),
@@ -348,11 +380,12 @@
             pltpu.VMEM((steps * wd, F), f32),
             pltpu.VMEM((steps, 2 * rows, F), bf16),
             pltpu.VMEM((NBINS * 3 * steps, 3 * steps * chd), bf16),
-            pltpu.VMEM((2, 3 * steps * chd, CHUNK), bf16),
+            pltpu.VMEM((3 * steps * chd, 2 * CHUNK), bf16),
             pltpu.VMEM((NBINS * 3 * steps, 128), f32),
             pltpu.VMEM((steps * wd, 128), f32),
-            pltpu.VMEM((units, 2, g2, 2, g4) + tail, f32),
-            pltpu.VMEM((units, g2, 2, g4) + tail, f32),
+            pltpu.VMEM((units, steps * bl, CHUNK), f32),
+            pltpu.VMEM((units, 2, g2, 2, g4) + tail, bf16),
+            pltpu.VMEM((units, g2, 2, g4) + tail, bf16),
             pltpu.VMEM((units, 2, g4) + tail, f32),
             pltpu.VMEM((units, g2, 2, g4) + tail, bf16),
             pltpu.VMEM((units, g2 - 1, 2, g4) + tail, bf16),
@@ -373,10 +406,7 @@
             collective_id=0, has_side_effects=True, vmem_limit_bytes=56 * 1024 * 1024
         ),
         name="stack",
-    )(x, srccol, kcol, cnt, jnp.asarray(edge), jnp.asarray(table))
-    out = jnp.transpose(out, (1, 0, 2)).reshape(steps, bl, lag_dev)
-    mirrored = jnp.roll(jnp.flip(out, axis=-1), 1, axis=-1)
-    return jnp.where(lax.axis_index("win") < blocks, mirrored, out)
+    )(x, sources, bin_rows[:, 0], jnp.asarray(edge), jnp.asarray(table))
 
 
 def solution(mesh):

time: 67.7 us -> 66.3 us (0.979)
  Pallas kernels: 56.5 us -> 60.6 us
  other arithmetic: 3.84 us -> 0 us
  local copies, waits for them, and re-layouts: 6.96 us -> 5.34 us
    pallas_call x1, Pallas kernels: 56.5 us -> 60.6 us  [shards(): pl.pallas_call(functools.partial(kernel, cfg), out_shape=jax.ShapeDtypeSt...]
    unnamed x2, local copies, waits for them, and re-layouts: 0.84 us -> 2.89 us
    select_n x3 -> x0, other arithmetic: 1.61 us -> none  [the longest x1 0.8 us: shards(): jnp.where(slots >= 0, slots + step_at + term_at, -1)]
    transpose x1 -> x0, local copies, waits for them, and re-layouts: 0.89 us -> none  [shards(): out = jnp.transpose(out, (1, 0, 2)).reshape(steps, bl, lag_dev)]
    broadcast_in_dim x2 -> x0, local copies, waits for them, and re-layouts: 0.73 us -> none  [the longest x1 0.7 us: shards(): cnt = jnp.broadcast_to(live, (nchan, steps * wd, 128)).astype(bf16)]
    unnamed x1 -> x0, other arithmetic: 0.73 us -> none
    reduce_sum x1 -> x0, other arithmetic: 0.72 us -> none  [shards(): jnp.sum((bin_rows[:, 0] >= 0).astype(f32), axis=-1)]
where the time goes in v2:
time: 66.3 us; the launch traced here: 66 us
  Pallas kernels  60.6 us (91%)
  local copies, waits for them, and re-layouts  5.34 us (8%)
    pallas_call x1, Pallas kernels, shards(): pl.pallas_call(functools.partial(kernel, cfg), out_shape=jax.ShapeDtypeSt...  60.6 us
    unnamed x2, local copies, waits for them, and re-layouts  2.89 us
    transpose x1, local copies, waits for them, and re-layouts, shards(): x = jnp.transpose(spectra, (2, 1, 0, 3)).reshape(2, rows, F)  2.44 us

profile of v2, /device:TPU:0, one launch (start us, length us, event | category | flops | bytes accessed | tf_op | source)
XLA Modules:
  0.0 66.0 jit_solution(8058539287605157619)
XLA Ops:
  0.0 1.4 %copy.7 = s32[4,1,32,3]{3,2,0,1:T(8,128)} copy(s32[4,1,32,3]{2,1,3,0:T(1,128)} %param.7) | data formatting | bytes 3072 | tf_op args[2]
  1.4 2.4 %copy.6 = bf16[2,4,48,1024]{3,2,1,0:T(8,128)(2,1)} copy(bf16[2,4,48,1024]{3,0,1,2:T(2,128)(2,1)} %bitcast.4) | data formatting | bytes 1572864 | tf_op jit(solution)/shard_map/transpose | solution.py:358
  3.9 60.6 %stack.1 = f32[4,4,1024]{2,1,0:T(4,128)} custom-call(bf16[2,192,1024]{2,1,0:T(8,128)(2,1)} %bitcast.3, s32[4]{0:T(128)} %sources_ref.1, s32[4,32,3]{2,1,0:T(8,128)} %bitcast.5, bf16[1024,256]{1,0:T(8,128)(2,1)} %constant.4.clone.edge_ref, bf16[8,2,1024,256]{3,2,1,0:T(8,128)(2,1)} %constant.5.clone.tab_hbm), custom_call_target="tpu_custom_call" | custom-call | tf_op jit(solution)/shard_map/stack/pallas_call | solution.py:367
  64.5 1.5 %copy.9 = f32[4,4,1024]{2,1,0:T(4,128)} copy(f32[4,4,1024]{2,1,0:T(4,128)} %stack.1) | data formatting | bytes 131072

commit v3 on v2

--- a/solution.py
+++ b/solution.py
@@ -77,7 +77,7 @@
     cfg,
     x_ref, sources_ref, bins_ref, edge_ref, tab_hbm,
     o_ref,
-    tab, sbuf, rsr, ag, wr_s, wi_s, sr_s, si_s, xs, wmat, ts, oe, traces, fin,
+    tab, sbuf, rsr, ag, wr_s, wi_s, sr_s, si_s, xs, wmat, ts, oe, traces, fin, res_a, res_b,
     p1, r1, a2, b2, r2, a3, b3, r3, a4, b4, r4,
     tab_sem, rs_s, rs_r, ag_s, ag_r, s1, q1, s2, q2, s3, q3, s4, q4,
 ):
@@ -130,20 +130,23 @@
         want = jnp.where(row // wd == s, (row % wd) * chd + loc, want)
     pick = jnp.where(col == want, 1.0, 0.0).astype(bf16)
     both = jnp.concatenate([dot(pick, x_ref[0]), dot(pick, x_ref[1])], axis=1).astype(bf16)
-    slots = bins_ref[...].reshape(steps * NBINS, MOST)
-    live = jnp.sum(jnp.where(slots >= 0, 1.0, 0.0), axis=1, keepdims=True)
-    live = jnp.broadcast_to(live, (steps * NBINS, 128)).astype(bf16)
-
-    def row_of(shape, dims):
+    slots = bins_ref[...].astype(f32)
+    live = jnp.where(slots >= 0.0, 1.0, 0.0).astype(bf16)
+
+    def bins_of(shape, dims):
         i = lax.broadcasted_iota(jnp.int32, shape, len(shape) - 2)
-        b = sum(lax.broadcasted_iota(jnp.int32, shape, d) * size for d, size in dims)
-        here = (i // bl) * NBINS + b * bl + i % bl
-        hit = lax.broadcasted_iota(jnp.int32, shape, len(shape) - 1) == here
-        return jnp.where(hit, 1.0, 0.0), i // bl
-
-    shape = (nchan, steps * bl, steps * NBINS)
-    chosen, _ = row_of(shape, [(0, 1)])
-    cnt = dot(chosen.reshape(nchan * steps * bl, steps * NBINS).astype(bf16), live).astype(bf16)
+        b = sum(lax.broadcasted_iota(jnp.int32, shape, d) * size for d, size in dims) * bl + i % bl
+        hit = lax.broadcasted_iota(jnp.int32, shape, len(shape) - 1) == b
+        return jnp.where(hit, 1.0, 0.0).reshape(-1, NBINS).astype(bf16), (i // bl).reshape(-1, NBINS)[:, 0:1]
+
+    def pick_slots(chosen, values):
+        return lax.dot_general(chosen, values, (((1,), (1,)), ((), ())), preferred_element_type=f32)
+
+    chosen, step = bins_of((nchan, steps * bl, NBINS), [(0, 1)])
+    cnt = pick_slots(chosen, live)
+    col = lax.broadcasted_iota(jnp.int32, cnt.shape, 1)
+    cnt = jnp.sum(jnp.where(col // MOST == step, cnt, 0.0), axis=1, keepdims=True)
+    cnt = jnp.broadcast_to(cnt, (nchan * steps * bl, 128)).astype(bf16)
     for d in range(nchan):
         sbuf[d, :, :piece] = both[:, d * piece : (d + 1) * piece]
         sbuf[d, :, piece:] = jnp.zeros((steps * wd, 128), bf16)
@@ -178,17 +181,18 @@
     for k in range(1, nchan):
         ag_copy(k).start()
 
-    shape = (2, g4, 3, steps * bl, steps * NBINS)
-    chosen, step = row_of(shape, [(0, 1), (1, 2)])
-    chosen = chosen.reshape(-1, steps * NBINS).astype(bf16)
-    offset = (step * 3 + lax.broadcasted_iota(jnp.int32, shape, 2)).astype(f32) * chd
-    offset = offset.reshape(-1, steps * NBINS)[:, 0:1]
-    slots_at = dot(chosen, slots.astype(f32).astype(bf16))
-    slots_at = jnp.where(slots_at >= 0.0, slots_at + offset, -1.0)
+    shape = (2, g4, 3, steps * bl, NBINS)
+    chosen, step = bins_of(shape, [(0, 1), (1, 2)])
+    term = lax.broadcasted_iota(jnp.int32, shape, 2).reshape(-1, NBINS)[:, 0:1]
+    offset = ((step * 3 + term) * chd).astype(f32)
+    slots_at = pick_slots(chosen, slots.astype(bf16))
     wcol = lax.broadcasted_iota(jnp.int32, wmat.shape, 1).astype(f32)
-    hit = wcol == slots_at[:, 0:1]
-    for k in range(1, MOST):
-        hit = hit | (wcol == slots_at[:, k : k + 1])
+    hit = wcol < 0.0
+    for k in range(MOST):
+        row_at = slots_at[:, k : k + 1]
+        for s in range(1, steps):
+            row_at = jnp.where(step == s, slots_at[:, s * MOST + k : s * MOST + k + 1], row_at)
+        hit = hit | (wcol == jnp.where(row_at >= 0.0, row_at + offset, -1.0))
     wmat[...] = jnp.where(hit, 1.0, 0.0).astype(bf16)
 
     for k in range(1, nchan):
@@ -207,32 +211,44 @@
         for s in range(steps):
             i = s * wd + w
             a, b = sr_s[i : i + 1, :], si_s[i : i + 1, :]
-            xs[s, here, :] = (wrw * a + wiw * b).astype(bf16)
-            xs[s, slice(rows + w * chd, rows + (w + 1) * chd), :] = (wiw * a - wrw * b).astype(bf16)
-
-    def add_terms(sign, s, re, im):
-        inv = lax.rsqrt(jnp.maximum(re * re + im * im, phase_floor * phase_floor))
-        for q, value in enumerate((re, re * inv, im * inv)):
-            total = value[:chd]
-            for w in range(1, wd):
-                total = total + value[w * chd : (w + 1) * chd]
-            first = (s * 3 + q) * chd
-            ts[first : first + chd, sign * CHUNK : (sign + 1) * CHUNK] = total.astype(bf16)
-
-    for s in range(steps):
-        res = dot(xs[s], edge_ref[...])
-        add_terms(1, s, res[:rows, :128] + res[rows:, 128:], res[rows:, :128] - res[:rows, 128:])
+            first = 2 * s * rows + w * chd
+            xs[first : first + chd, :] = (wrw * a + wiw * b).astype(bf16)
+            xs[first + rows : first + rows + chd, :] = (wiw * a - wrw * b).astype(bf16)
+
+    tile = 16
+
+    def add_terms(res, signs):
+        for s in range(steps):
+            for r in range(0, chd, tile):
+                sums = [None] * 6
+                for w in range(wd):
+                    top = 2 * s * rows + w * chd + r
+                    a, c = res[top : top + tile, :CHUNK], res[top : top + tile, CHUNK:]
+                    top += rows
+                    d, b = res[top : top + tile, :CHUNK], res[top : top + tile, CHUNK:]
+                    for sign in signs:
+                        re, im = (a + b, d - c) if sign else (a - b, c + d)
+                        inv = lax.rsqrt(jnp.maximum(re * re + im * im, phase_floor * phase_floor))
+                        for q, value in enumerate((re, re * inv, im * inv)):
+                            n = sign * 3 + q
+                            sums[n] = value if w == 0 else sums[n] + value
+                for sign in signs:
+                    for q in range(3):
+                        first = (s * 3 + q) * chd + r
+                        at = slice(sign * CHUNK, (sign + 1) * CHUNK)
+                        ts[first : first + tile, at] = sums[sign * 3 + q].astype(bf16)
+
+    res_a[...] = dot(xs[...], edge_ref[...])
+    add_terms(res_a, (1,))
     oe[...] = dot(wmat[...], ts[:, CHUNK:])
 
-    def compute(u, m):
-        res = dot(xs[0], tab[u, m])
-        for s in range(steps):
-            later = dot(xs[s + 1], tab[u, m]) if s + 1 < steps else None
-            a, c = res[:rows, :CHUNK], res[:rows, CHUNK:]
-            d, b = res[rows:, :CHUNK], res[rows:, CHUNK:]
-            add_terms(0, s, a - b, c + d)
-            add_terms(1, s, a + b, d - c)
-            res = later
+    both_res = (res_a, res_b)
+
+    def correlate(u, m):
+        both_res[m % 2][...] = dot(xs[...], tab[u, m])
+
+    def bin_sums(u, m):
+        add_terms(both_res[m % 2], (0, 1))
         pos = blocks + m
         neg = blocks - 1 - m
         part = p1.shape[3:]
@@ -297,13 +313,30 @@
         count = traces[:n, :]
         fin[u] = lin * lax.rsqrt(count) * ((pr * pr + pi * pi) / count)
 
+    table_copy(0).wait()
+    for m in range(blocks):
+        correlate(0, m)
+        if m:
+            bin_sums(0, m - 1)
+
     def turn(v, carry):
         @pl.when(v < units)
         def _():
             table_copy(v).wait()
-            compute(v, 0)
-
-        @pl.when((v >= 1) & (v < units + 1))
+            for m in range(blocks):
+                correlate(v, m)
+                if m:
+                    bin_sums(v, m - 1)
+                else:
+                    bin_sums(v - 1, blocks - 1)
+                    copy1(v - 1).start()
+
+        @pl.when(v == units)
+        def _():
+            bin_sums(v - 1, blocks - 1)
+            copy1(v - 1).start()
+
+        @pl.when(v < units + 1)
         def _():
             stage2(v - 1)
 
@@ -319,15 +352,9 @@
         def _():
             stage5(v - 4)
 
-        @pl.when(v < units)
-        def _():
-            for m in range(1, blocks):
-                compute(v, m)
-            copy1(v).start()
-
         return carry
 
-    lax.fori_loop(0, units + 4, turn, 0)
+    lax.fori_loop(1, units + 4, turn, 0)
 
     ri = lax.broadcasted_iota(jnp.int32, (CHUNK, CHUNK), 0)
     rj = lax.broadcasted_iota(jnp.int32, (CHUNK, CHUNK), 1)
@@ -342,8 +369,7 @@
         value = dot(hi, flip) + dot(mid, flip) + dot(low, flip)
         value = jnp.where(lane == 0, fin[(units - u) % units], value)
         value = jnp.where(lane * 0 + me_w < blocks, value, fin[u])
-        for s in range(steps):
-            o_ref[s, :, u * CHUNK : (u + 1) * CHUNK] = value[s * bl : (s + 1) * bl]
+        o_ref[:, u * CHUNK : (u + 1) * CHUNK] = value
 
 
 def shards(spectra, sources, bin_rows):
@@ -364,9 +390,10 @@
     cfg = (nchan, nwin, steps, wd, chd, units, blocks)
     dma = pltpu.SemaphoreType.DMA
     vmem = pl.BlockSpec(memory_space=pltpu.VMEM)
-    return pl.pallas_call(
+    slots = jnp.transpose(bin_rows, (0, 3, 1, 2)).reshape(steps * MOST, NBINS)
+    out = pl.pallas_call(
         functools.partial(kernel, cfg),
-        out_shape=jax.ShapeDtypeStruct((steps, bl, lag_dev), f32),
+        out_shape=jax.ShapeDtypeStruct((steps * bl, lag_dev), f32),
         in_specs=[vmem, pl.BlockSpec(memory_space=pltpu.SMEM), vmem, vmem] + [pl.BlockSpec(memory_space=pl.ANY)],
         out_specs=vmem,
         scratch_shapes=[
@@ -378,12 +405,14 @@
             pltpu.VMEM((rows, F), bf16),
             pltpu.VMEM((steps * wd, F), f32),
             pltpu.VMEM((steps * wd, F), f32),
-            pltpu.VMEM((steps, 2 * rows, F), bf16),
+            pltpu.VMEM((steps * 2 * rows, F), bf16),
             pltpu.VMEM((NBINS * 3 * steps, 3 * steps * chd), bf16),
             pltpu.VMEM((3 * steps * chd, 2 * CHUNK), bf16),
             pltpu.VMEM((NBINS * 3 * steps, 128), f32),
             pltpu.VMEM((steps * wd, 128), f32),
             pltpu.VMEM((units, steps * bl, CHUNK), f32),
+            pltpu.VMEM((steps * 2 * rows, 2 * CHUNK), f32),
+            pltpu.VMEM((steps * 2 * rows, 2 * CHUNK), f32),
             pltpu.VMEM((units, 2, g2, 2, g4) + tail, bf16),
             pltpu.VMEM((units, g2, 2, g4) + tail, bf16),
             pltpu.VMEM((units, 2, g4) + tail, f32),
@@ -406,7 +435,8 @@
             collective_id=0, has_side_effects=True, vmem_limit_bytes=56 * 1024 * 1024
         ),
         name="stack",
-    )(x, sources, bin_rows[:, 0], jnp.asarray(edge), jnp.asarray(table))
+    )(x, sources, slots, jnp.asarray(edge), jnp.asarray(table))
+    return out.reshape(steps, bl, lag_dev)
 
 
 def solution(mesh):

time: 66.3 us -> 69.4 us (1.047)
  Pallas kernels: 60.6 us -> 63.9 us
    pallas_call x1, Pallas kernels: 60.6 us -> 63.9 us  [shards(): pl.pallas_call(functools.partial(kernel, cfg), out_shape=jax.ShapeDtypeSt...]
    unnamed x2, local copies, waits for them, and re-layouts: 2.89 us -> 0.69 us
    reshape x0 -> x2, local copies, waits for them, and re-layouts: none -> 2.1 us  [the longest x1 1.49 us: shards(): return out.reshape(steps, bl, lag_dev)]
where the time goes in v3:
time: 69.4 us; the launch traced here: 69.1 us
  Pallas kernels  63.9 us (92%)
  local copies, waits for them, and re-layouts  5.26 us (8%)
    pallas_call x1, Pallas kernels, shards(): pl.pallas_call(functools.partial(kernel, cfg), out_shape=jax.ShapeDtypeSt...  63.9 us
    transpose x1, local copies, waits for them, and re-layouts, shards(): x = jnp.transpose(spectra, (2, 1, 0, 3)).reshape(2, rows, F)  2.44 us
    reshape x1, local copies, waits for them, and re-layouts, shards(): return out.reshape(steps, bl, lag_dev)  1.49 us

profile of v3, /device:TPU:0, one launch (start us, length us, event | category | flops | bytes accessed | tf_op | source)
XLA Modules:
  0.0 69.1 jit_solution(10177341414323253510)
XLA Ops:
  0.0 0.0 copy-start
  0.0 0.7 copy-done
  0.7 0.6 reshape.10.bins_ref
  1.3 2.4 %copy.6 = bf16[2,4,48,1024]{3,2,1,0:T(8,128)(2,1)} copy(bf16[2,4,48,1024]{3,0,1,2:T(2,128)(2,1)} %bitcast.5) | data formatting | bytes 1572864 | tf_op jit(solution)/shard_map/transpose | solution.py:384
  3.8 63.9 %stack.1 = f32[16,1024]{1,0:T(8,128)} custom-call(bf16[2,192,1024]{2,1,0:T(8,128)(2,1)} %bitcast.4, s32[4]{0:T(128)} %sources_ref.1, s32[12,32]{1,0:T(8,128)} %reshape.10.bins_ref, bf16[1024,256]{1,0:T(8,128)(2,1)} %constant.4.clone.edge_ref, bf16[8,2,1024,256]{3,2,1,0:T(8,128)(2,1)} %constant.5.clone.tab_hbm), custom_call_target="tpu_custom_call" | custom-call | tf_op jit(solution)/shard_map/stack/pallas_call | solution.py:394
  67.7 1.5 %reshape.11 = f32[4,4,1024]{2,1,0:T(4,128)} reshape(f32[16,1024]{1,0:T(8,128)} %stack.1) | data formatting | bytes 131072 | tf_op jit(solution)/shard_map/reshape | solution.py:439
  (1 shorter events, 0.0 us)
Async XLA Ops:
  0.0 0.7 %copy-start = (s32[4,1,32,3]{2,1,3,0:T(1,128)S(1)}, s32[4,1,32,3]{2,1,3,0:T(1,128)}, u32[]{:S(2)}) copy-start(s32[4,1,32,3]{2,1,3,0:T(1,128)} %param.7) | copy-start | bytes 4612

commit v4 on v3

--- a/solution.py
+++ b/solution.py
@@ -28,27 +28,22 @@
 
 
 def lag_tables(lag_dev):
-    blocks = LMAX // lag_dev
+    blocks = LMAX // 2 // lag_dev
     units = lag_dev // CHUNK
     freq = F0 + np.arange(F, dtype=np.int64)
 
     def trig(lags):
         turn = (freq[:, None] * lags[None, :]) % NFFT
         angle = turn * (2.0 * np.pi / NFFT)
-        scale = F ** -0.5
-        return np.cos(angle).astype(ml_dtypes.bfloat16), np.sin(angle).astype(ml_dtypes.bfloat16), scale
-
-    table = np.zeros((units, blocks, F, 2 * CHUNK), ml_dtypes.bfloat16)
-    for u in range(units):
-        for m in range(blocks):
-            cosine, sine, scale = trig(m * lag_dev + u * CHUNK + np.arange(CHUNK))
-            both = np.concatenate([cosine, sine], axis=1).astype(np.float32) * scale
-            table[u, m] = both.astype(ml_dtypes.bfloat16)
-    edge = np.zeros((F, 256), np.float32)
-    cosine, sine, scale = trig((np.arange(blocks) + 1) * lag_dev)
-    edge[:, :blocks] = cosine.astype(np.float32) * scale
-    edge[:, 128 : 128 + blocks] = sine.astype(np.float32) * scale
-    return table, edge.astype(ml_dtypes.bfloat16)
+        both = np.zeros((F, 256), np.float32)
+        both[:, : lags.size] = np.cos(angle).astype(ml_dtypes.bfloat16)
+        both[:, CHUNK : CHUNK + lags.size] = np.sin(angle).astype(ml_dtypes.bfloat16)
+        both = (both * F ** -0.5).astype(ml_dtypes.bfloat16)
+        return np.stack([both[m::4] for m in range(4)])
+
+    starts = [[m * lag_dev + u * CHUNK for m in range(blocks)] for u in range(units)]
+    table = np.stack([np.stack([trig(t + np.arange(CHUNK)) for t in at]) for at in starts])
+    return table, trig((np.arange(blocks) + 1) * lag_dev)
 
 
 def dot(a, b):
@@ -130,8 +125,7 @@
         want = jnp.where(row // wd == s, (row % wd) * chd + loc, want)
     pick = jnp.where(col == want, 1.0, 0.0).astype(bf16)
     both = jnp.concatenate([dot(pick, x_ref[0]), dot(pick, x_ref[1])], axis=1).astype(bf16)
-    slots = bins_ref[...].astype(f32)
-    live = jnp.where(slots >= 0.0, 1.0, 0.0).astype(bf16)
+    slots = [bins_ref[s].astype(f32) for s in range(steps)]
 
     def bins_of(shape, dims):
         i = lax.broadcasted_iota(jnp.int32, shape, len(shape) - 2)
@@ -143,9 +137,10 @@
         return lax.dot_general(chosen, values, (((1,), (1,)), ((), ())), preferred_element_type=f32)
 
     chosen, step = bins_of((nchan, steps * bl, NBINS), [(0, 1)])
-    cnt = pick_slots(chosen, live)
-    col = lax.broadcasted_iota(jnp.int32, cnt.shape, 1)
-    cnt = jnp.sum(jnp.where(col // MOST == step, cnt, 0.0), axis=1, keepdims=True)
+    cnt = jnp.zeros(step.shape, f32)
+    for s in range(steps):
+        live = pick_slots(chosen, jnp.where(slots[s] >= 0.0, 1.0, 0.0).astype(bf16))
+        cnt = jnp.where(step == s, jnp.sum(live, axis=1, keepdims=True), cnt)
     cnt = jnp.broadcast_to(cnt, (nchan * steps * bl, 128)).astype(bf16)
     for d in range(nchan):
         sbuf[d, :, :piece] = both[:, d * piece : (d + 1) * piece]
@@ -168,8 +163,11 @@
     bj = lax.broadcasted_iota(jnp.int32, (768, 256), 1)
     band = jnp.where(jnp.abs(bi - 256 - bj) <= HW, 1.0, 0.0).astype(bf16)
     wr, wi = whiten(x_ref[0].astype(f32), x_ref[1].astype(f32), band)
-    wr_s[...] = wr
-    wi_s[...] = wi
+    pi_ = lax.broadcasted_iota(jnp.int32, (F, F), 0)
+    pj = lax.broadcasted_iota(jnp.int32, (F, F), 1)
+    order = jnp.where(pi_ == (pj % 256) * 4 + pj // 256, 1.0, 0.0).astype(bf16)
+    wr_s[...] = dot(wr, order).astype(bf16)
+    wi_s[...] = dot(wi, order).astype(bf16)
 
     for k in range(1, nchan):
         rs_copy(k).wait()
@@ -185,14 +183,14 @@
     chosen, step = bins_of(shape, [(0, 1), (1, 2)])
     term = lax.broadcasted_iota(jnp.int32, shape, 2).reshape(-1, NBINS)[:, 0:1]
     offset = ((step * 3 + term) * chd).astype(f32)
-    slots_at = pick_slots(chosen, slots.astype(bf16))
+    slots_at = pick_slots(chosen, slots[0].astype(bf16))
+    for s in range(1, steps):
+        slots_at = jnp.where(step == s, pick_slots(chosen, slots[s].astype(bf16)), slots_at)
+    slots_at = jnp.where(slots_at >= 0.0, slots_at + offset, -1.0)
     wcol = lax.broadcasted_iota(jnp.int32, wmat.shape, 1).astype(f32)
     hit = wcol < 0.0
     for k in range(MOST):
-        row_at = slots_at[:, k : k + 1]
-        for s in range(1, steps):
-            row_at = jnp.where(step == s, slots_at[:, s * MOST + k : s * MOST + k + 1], row_at)
-        hit = hit | (wcol == jnp.where(row_at >= 0.0, row_at + offset, -1.0))
+        hit = hit | (wcol == slots_at[:, k : k + 1])
     wmat[...] = jnp.where(hit, 1.0, 0.0).astype(bf16)
 
     for k in range(1, nchan):
@@ -201,8 +199,8 @@
     sre = jnp.concatenate([ag[d] for d in range(half)], axis=1).astype(f32)
     sim = jnp.concatenate([ag[d] for d in range(half, nchan)], axis=1).astype(f32)
     sr, si = whiten(sre, sim, band)
-    sr_s[...] = sr.astype(f32)
-    si_s[...] = si.astype(f32)
+    sr_s[...] = dot(sr, order)
+    si_s[...] = dot(si, order)
 
     for w in range(wd):
         here = slice(w * chd, (w + 1) * chd)
@@ -215,48 +213,74 @@
             xs[first : first + chd, :] = (wrw * a + wiw * b).astype(bf16)
             xs[first + rows : first + rows + chd, :] = (wiw * a - wrw * b).astype(bf16)
 
-    tile = 16
-
-    def add_terms(res, signs):
-        for s in range(steps):
-            for r in range(0, chd, tile):
-                sums = [None] * 6
-                for w in range(wd):
-                    top = 2 * s * rows + w * chd + r
-                    a, c = res[top : top + tile, :CHUNK], res[top : top + tile, CHUNK:]
-                    top += rows
-                    d, b = res[top : top + tile, :CHUNK], res[top : top + tile, CHUNK:]
-                    for sign in signs:
-                        re, im = (a + b, d - c) if sign else (a - b, c + d)
-                        inv = lax.rsqrt(jnp.maximum(re * re + im * im, phase_floor * phase_floor))
-                        for q, value in enumerate((re, re * inv, im * inv)):
-                            n = sign * 3 + q
-                            sums[n] = value if w == 0 else sums[n] + value
-                for sign in signs:
+    tile = 8
+    lanes = (slice(0, CHUNK), slice(CHUNK, 2 * CHUNK))
+
+    def lag_values(res, top, outs):
+        g, h = [], []
+        for m in range(4):
+            a, c = res[m, top : top + tile, lanes[0]], res[m, top : top + tile, lanes[1]]
+            d, b = res[m, top + rows : top + rows + tile, lanes[0]], res[m, top + rows : top + rows + tile, lanes[1]]
+            g.append((a - b, c + d))
+            h.append((a + b, d - c))
+        values = {}
+        for parts, plain, turned, sign in ((g, 0, 1, 1), (h, 2, 3, -1)):
+            (r0, i0), (r1, i1), (r2, i2), (r3, i3) = parts
+            if plain in outs:
+                values[plain] = (r0 + r2) + (r1 + r3), (i0 + i2) + (i1 + i3)
+            if turned in outs:
+                ro, io = r1 - r3, i1 - i3
+                if sign > 0:
+                    values[turned] = (r0 - r2) + io, (i0 - i2) - ro
+                else:
+                    values[turned] = (r0 - r2) - io, (i0 - i2) + ro
+        return values
+
+    def add_terms(res, h, outs):
+        for k in range(steps // 2):
+            for r in range(0, chd, 2 * tile):
+                halves = []
+                for r8 in (r, r + tile):
+                    sums = {}
+                    for w in range(wd):
+                        values = lag_values(res, 2 * k * rows + w * chd + r8, outs)
+                        for out in outs:
+                            re, im = values[out]
+                            inv = lax.rsqrt(jnp.maximum(re * re + im * im, phase_floor * phase_floor))
+                            for q, value in enumerate((re, re * inv, im * inv)):
+                                sums[out, q] = value if w == 0 else sums[out, q] + value
+                    halves.append(sums)
+                for out in outs:
                     for q in range(3):
-                        first = (s * 3 + q) * chd + r
-                        at = slice(sign * CHUNK, (sign + 1) * CHUNK)
-                        ts[first : first + tile, at] = sums[sign * 3 + q].astype(bf16)
-
-    res_a[...] = dot(xs[...], edge_ref[...])
-    add_terms(res_a, (1,))
-    oe[...] = dot(wmat[...], ts[:, CHUNK:])
+                        first = ((h * (steps // 2) + k) * 3 + q) * chd + r
+                        value = jnp.concatenate([half[out, q] for half in halves], axis=0)
+                        ts[first : first + 2 * tile, out * CHUNK : (out + 1) * CHUNK] = value.astype(bf16)
 
     both_res = (res_a, res_b)
-
-    def correlate(u, m):
-        both_res[m % 2][...] = dot(xs[...], tab[u, m])
-
-    def bin_sums(u, m):
-        add_terms(both_res[m % 2], (0, 1))
-        pos = blocks + m
-        neg = blocks - 1 - m
+    part_rows = steps * rows
+
+    def correlate(table, h):
+        for m in range(4):
+            both_res[h][m] = dot(xs[h * part_rows : (h + 1) * part_rows, m * 256 : (m + 1) * 256], table[m])
+
+    for h in range(2):
+        correlate(edge_ref, h)
+        add_terms(both_res[h], h, (2, 3))
+    oe[...] = dot(wmat[...], ts[:, 2 * CHUNK :])
+
+    def bin_sums(u, m, h):
+        add_terms(both_res[h], h, (0, 1, 2, 3))
+        if h == 0:
+            return
         part = p1.shape[3:]
         value = dot(wmat[...], ts[...])
-        p1[u, pos % 2, pos // 2] = value[:, :CHUNK].reshape(part).astype(bf16)
         lane = lax.broadcasted_iota(jnp.int32, (wmat.shape[0], CHUNK), 1)
-        mirror = jnp.where((lane + u) == 0, oe[:, m : m + 1], value[:, CHUNK:])
-        p1[u, neg % 2, neg // 2] = mirror.reshape(part).astype(bf16)
+        for out, w in enumerate((nwin // 2 + m, m, nwin // 2 - 1 - m, nwin - 1 - m)):
+            piece_out = value[:, out * CHUNK : (out + 1) * CHUNK]
+            if out >= 2:
+                at = (out - 2) * CHUNK + m
+                piece_out = jnp.where((lane + u) == 0, oe[:, at : at + 1], piece_out)
+            p1[u, w % 2, w // 2] = piece_out.reshape(part).astype(bf16)
 
     def copy1(u):
         return remote(p1.at[u, 1 - w1], r1.at[u], s1.at[u], q1.at[u], dev1())
@@ -313,27 +337,28 @@
         count = traces[:n, :]
         fin[u] = lin * lax.rsqrt(count) * ((pr * pr + pi * pi) / count)
 
+    jobs = [(m, h) for m in range(blocks) for h in range(2)]
     table_copy(0).wait()
-    for m in range(blocks):
-        correlate(0, m)
-        if m:
-            bin_sums(0, m - 1)
+    for n, (m, h) in enumerate(jobs):
+        correlate(tab.at[0, m], h)
+        if n:
+            bin_sums(0, *jobs[n - 1])
 
     def turn(v, carry):
         @pl.when(v < units)
         def _():
             table_copy(v).wait()
-            for m in range(blocks):
-                correlate(v, m)
-                if m:
-                    bin_sums(v, m - 1)
+            for n, (m, h) in enumerate(jobs):
+                correlate(tab.at[v, m], h)
+                if n:
+                    bin_sums(v, *jobs[n - 1])
                 else:
-                    bin_sums(v - 1, blocks - 1)
+                    bin_sums(v - 1, *jobs[-1])
                     copy1(v - 1).start()
 
         @pl.when(v == units)
         def _():
-            bin_sums(v - 1, blocks - 1)
+            bin_sums(v - 1, *jobs[-1])
             copy1(v - 1).start()
 
         @pl.when(v < units + 1)
@@ -368,7 +393,7 @@
         low = (rest - mid.astype(f32)).astype(bf16)
         value = dot(hi, flip) + dot(mid, flip) + dot(low, flip)
         value = jnp.where(lane == 0, fin[(units - u) % units], value)
-        value = jnp.where(lane * 0 + me_w < blocks, value, fin[u])
+        value = jnp.where((lane * 0 + me_w // blocks) % 2 == 1, value, fin[u])
         o_ref[:, u * CHUNK : (u + 1) * CHUNK] = value
 
 
@@ -377,7 +402,7 @@
     steps = sources.shape[0]
     nchan, nwin = lax.axis_size("chan"), lax.axis_size("win")
     lag_dev = LAGS // nwin
-    units, blocks = lag_dev // CHUNK, nwin // 2
+    units, blocks = lag_dev // CHUNK, nwin // 4
     bl = NBINS // nchan
     rows = wd * chd
     g2, g4 = nwin // 2, nchan // 2
@@ -390,14 +415,14 @@
     cfg = (nchan, nwin, steps, wd, chd, units, blocks)
     dma = pltpu.SemaphoreType.DMA
     vmem = pl.BlockSpec(memory_space=pltpu.VMEM)
-    slots = jnp.transpose(bin_rows, (0, 3, 1, 2)).reshape(steps * MOST, NBINS)
+    slots = jnp.transpose(bin_rows[:, 0], (0, 2, 1))
     out = pl.pallas_call(
         functools.partial(kernel, cfg),
         out_shape=jax.ShapeDtypeStruct((steps * bl, lag_dev), f32),
         in_specs=[vmem, pl.BlockSpec(memory_space=pltpu.SMEM), vmem, vmem] + [pl.BlockSpec(memory_space=pl.ANY)],
         out_specs=vmem,
         scratch_shapes=[
-            pltpu.VMEM((units, blocks, F, 2 * CHUNK), bf16),
+            pltpu.VMEM((units, blocks, 4, F // 4, 2 * CHUNK), bf16),
             pltpu.VMEM((nchan, steps * wd, piece + 128), bf16),
             pltpu.VMEM((nchan - 1, steps * wd, piece + 128), bf16),
             pltpu.VMEM((nchan, steps * wd, piece), bf16),
@@ -407,12 +432,12 @@
             pltpu.VMEM((steps * wd, F), f32),
             pltpu.VMEM((steps * 2 * rows, F), bf16),
             pltpu.VMEM((NBINS * 3 * steps, 3 * steps * chd), bf16),
-            pltpu.VMEM((3 * steps * chd, 2 * CHUNK), bf16),
-            pltpu.VMEM((NBINS * 3 * steps, 128), f32),
+            pltpu.VMEM((3 * steps * chd, 4 * CHUNK), bf16),
+            pltpu.VMEM((NBINS * 3 * steps, 2 * CHUNK), f32),
             pltpu.VMEM((steps * wd, 128), f32),
             pltpu.VMEM((units, steps * bl, CHUNK), f32),
-            pltpu.VMEM((steps * 2 * rows, 2 * CHUNK), f32),
-            pltpu.VMEM((steps * 2 * rows, 2 * CHUNK), f32),
+            pltpu.VMEM((4, steps * rows, 2 * CHUNK), f32),
+            pltpu.VMEM((4, steps * rows, 2 * CHUNK), f32),
             pltpu.VMEM((units, 2, g2, 2, g4) + tail, bf16),
             pltpu.VMEM((units, g2, 2, g4) + tail, bf16),
             pltpu.VMEM((units, 2, g4) + tail, f32),

time: 69.4 us -> 65.9 us (0.950)
  Pallas kernels: 63.9 us -> 60.4 us
    pallas_call x1, Pallas kernels: 63.9 us -> 60.4 us  [shards(): pl.pallas_call(functools.partial(kernel, cfg), out_shape=jax.ShapeDtypeSt...]
    squeeze x0 -> x1, local copies, waits for them, and re-layouts: none -> 1.29 us  [shards(): slots = jnp.transpose(bin_rows[:, 0], (0, 2, 1))]
where the time goes in v4:
time: 65.9 us; the launch traced here: 65.7 us
  Pallas kernels  60.4 us (92%)
  local copies, waits for them, and re-layouts  5.22 us (8%)
    pallas_call x1, Pallas kernels, shards(): pl.pallas_call(functools.partial(kernel, cfg), out_shape=jax.ShapeDtypeSt...  60.4 us
    transpose x1, local copies, waits for them, and re-layouts, shards(): x = jnp.transpose(spectra, (2, 1, 0, 3)).reshape(2, rows, F)  2.44 us
    reshape x1, local copies, waits for them, and re-layouts, shards(): return out.reshape(steps, bl, lag_dev)  1.49 us

profile of v4, /device:TPU:0, one launch (start us, length us, event | category | flops | bytes accessed | tf_op | source)
XLA Modules:
  0.0 65.7 jit_solution(6407834985419088476)
XLA Ops:
  0.0 1.3 %copy.12 = s32[4,1,32,3]{2,3,0,1:T(4,128)} copy(s32[4,1,32,3]{2,1,3,0:T(1,128)} %param.7) | data formatting | bytes 3072 | tf_op jit(solution)/shard_map/squeeze | solution.py:418
  1.3 2.4 %copy.7 = bf16[2,4,48,1024]{3,2,1,0:T(8,128)(2,1)} copy(bf16[2,4,48,1024]{3,0,1,2:T(2,128)(2,1)} %bitcast.9) | data formatting | bytes 1572864 | tf_op jit(solution)/shard_map/transpose | solution.py:409
  3.7 60.4 %stack.1 = f32[16,1024]{1,0:T(8,128)} custom-call(bf16[2,192,1024]{2,1,0:T(8,128)(2,1)} %bitcast.8, s32[4]{0:T(128)} %sources_ref.1, s32[4,3,32]{2,1,0:T(4,128)} %bitcast.10, bf16[4,256,256]{2,1,0:T(8,128)(2,1)} %constant.4.clone.edge_ref, bf16[8,1,4,256,256]{4,3,2,1,0:T(8,128)(2,1)} %constant.5.clone.tab_hbm), custom_call_target="tpu_custom_call" | custom-call | tf_op jit(solution)/shard_map/stack/pallas_call | solution.py:419
  64.2 1.5 %reshape.7 = f32[4,4,1024]{2,1,0:T(4,128)} reshape(f32[16,1024]{1,0:T(8,128)} %stack.1) | data formatting | bytes 131072 | tf_op jit(solution)/shard_map/reshape | solution.py:464

commit v5 on v4

--- a/solution.py
+++ b/solution.py
@@ -73,7 +73,7 @@
     x_ref, sources_ref, bins_ref, edge_ref, tab_hbm,
     o_ref,
     tab, sbuf, rsr, ag, wr_s, wi_s, sr_s, si_s, xs, wmat, ts, oe, traces, fin, res_a, res_b,
-    p1, r1, a2, b2, r2, a3, b3, r3, a4, b4, r4,
+    p1, r1, a2, b2, r2, a3, b3, r3, a4, b4, r4, a3o, b3o, r3o, b2o, r2o,
     tab_sem, rs_s, rs_r, ag_s, ag_r, s1, q1, s2, q2, s3, q3, s4, q4,
 ):
     nchan, nwin, steps, wd, chd, units, blocks = cfg
@@ -165,7 +165,7 @@
     wr, wi = whiten(x_ref[0].astype(f32), x_ref[1].astype(f32), band)
     pi_ = lax.broadcasted_iota(jnp.int32, (F, F), 0)
     pj = lax.broadcasted_iota(jnp.int32, (F, F), 1)
-    order = jnp.where(pi_ == (pj % 256) * 4 + pj // 256, 1.0, 0.0).astype(bf16)
+    order = jnp.where(pi_ == (pj & 255) * 4 + (pj >> 8), 1.0, 0.0).astype(bf16)
     wr_s[...] = dot(wr, order).astype(bf16)
     wi_s[...] = dot(wi, order).astype(bf16)
 
@@ -298,15 +298,38 @@
             b4.at[u, lax.rem(c2 + k, g4)], r4.at[u, k - 1], s4.at[u, k - 1], q4.at[u, k - 1], dev4(k)
         )
 
-    def stage2(u):
-        copy1(u).wait()
+    def copy2_odd(u, k):
+        return remote(
+            b2o.at[u, lax.rem(w2 + k, g2)], r2o.at[u, k - 1], s2.at[u, k - 1], q2.at[u, k - 1], dev2(k)
+        )
+
+    def copy3_odd(u):
+        return remote(b3o.at[u, 1 - c1], r3o.at[u], s3.at[u], q3.at[u], dev3())
+
+    def by_parity(u, even, odd):
+        pl.when(lax.rem(u, 2) == 0)(lambda: even(u))
+        pl.when(lax.rem(u, 2) == 1)(lambda: odd(u))
+
+    def stage2_even(u):
         for i in range(g2):
             b2[u, i] = (p1[u, w1, i].astype(f32) + r1[u, i].astype(f32)).astype(bf16)
         for k in range(1, g2):
             copy2(u, k).start()
         a2[u] = p1[u, w1, w2].astype(f32) + r1[u, w2].astype(f32)
 
-    def stage3(u):
+    def stage2_odd(u):
+        for i in range(g2):
+            for c in range(2):
+                b3o[u, c, i] = (p1[u, w1, i, c].astype(f32) + r1[u, i, c].astype(f32)).astype(bf16)
+        copy3_odd(u).start()
+        for i in range(g2):
+            a3o[u, i] = p1[u, w1, i, c1].astype(f32) + r1[u, i, c1].astype(f32)
+
+    def stage2(u):
+        copy1(u).wait()
+        by_parity(u, stage2_even, stage2_odd)
+
+    def stage3_even(u):
         for k in range(1, g2):
             copy2(u, k).wait()
         for i in range(2):
@@ -317,12 +340,37 @@
             b3[u, i] = total.astype(bf16)
         copy3(u).start()
 
-    def stage4(u):
+    def stage3_odd(u):
+        copy3_odd(u).wait()
+        for i in range(g2):
+            total = a3o[u, i] + r3o[u, i].astype(f32)
+            a3o[u, i] = total
+            b2o[u, i] = total.astype(bf16)
+        for k in range(1, g2):
+            copy2_odd(u, k).start()
+
+    def stage3(u):
+        by_parity(u, stage3_even, stage3_odd)
+
+    def stage4_even(u):
         copy3(u).wait()
         for i in range(g4):
             total = a3[u, c1, i] + r3[u, i].astype(f32)
             a4[u, i] = total
             b4[u, i] = total.astype(bf16)
+
+    def stage4_odd(u):
+        for k in range(1, g2):
+            copy2_odd(u, k).wait()
+        for i in range(g4):
+            total = a3o[u, w2, i]
+            for k in range(1, g2):
+                total = total + r2o[u, k - 1, i].astype(f32)
+            a4[u, i] = total
+            b4[u, i] = total.astype(bf16)
+
+    def stage4(u):
+        by_parity(u, stage4_even, stage4_odd)
         for k in range(1, g4):
             copy4(u, k).start()
 
@@ -361,25 +409,14 @@
             bin_sums(v - 1, *jobs[-1])
             copy1(v - 1).start()
 
-        @pl.when(v < units + 1)
-        def _():
-            stage2(v - 1)
-
-        @pl.when((v >= 2) & (v < units + 2))
-        def _():
-            stage3(v - 2)
-
-        @pl.when((v >= 3) & (v < units + 3))
-        def _():
-            stage4(v - 3)
-
-        @pl.when(v >= 4)
-        def _():
-            stage5(v - 4)
+        for stage, lag in ((stage2, 1), (stage3, 3), (stage4, 5), (stage5, 7)):
+            @pl.when((v >= lag) & (v < units + lag))
+            def _(stage=stage, lag=lag):
+                stage(v - lag)
 
         return carry
 
-    lax.fori_loop(1, units + 4, turn, 0)
+    lax.fori_loop(1, units + 7, turn, 0)
 
     ri = lax.broadcasted_iota(jnp.int32, (CHUNK, CHUNK), 0)
     rj = lax.broadcasted_iota(jnp.int32, (CHUNK, CHUNK), 1)
@@ -449,6 +486,11 @@
             pltpu.VMEM((units, g4) + tail, f32),
             pltpu.VMEM((units, g4) + tail, bf16),
             pltpu.VMEM((units, g4 - 1) + tail, bf16),
+            pltpu.VMEM((units, g2, g4) + tail, f32),
+            pltpu.VMEM((units, 2, g2, g4) + tail, bf16),
+            pltpu.VMEM((units, g2, g4) + tail, bf16),
+            pltpu.VMEM((units, g2, g4) + tail, bf16),
+            pltpu.VMEM((units, g2 - 1, g4) + tail, bf16),
             dma((units,)),
             dma((nchan - 1,)), dma((nchan - 1,)), dma((nchan - 1,)), dma((nchan - 1,)),
             dma((units,)), dma((units,)),

time: 65.9 us -> 60.4 us (0.917)
  Pallas kernels: 60.4 us -> 54.9 us
    pallas_call x1, Pallas kernels: 60.4 us -> 54.9 us  [shards(): pl.pallas_call(functools.partial(kernel, cfg), out_shape=jax.ShapeDtypeSt...]
where the time goes in v5:
time: 60.4 us; the launch traced here: 60.2 us
  Pallas kernels  54.9 us (91%)
  local copies, waits for them, and re-layouts  5.22 us (9%)
    pallas_call x1, Pallas kernels, shards(): pl.pallas_call(functools.partial(kernel, cfg), out_shape=jax.ShapeDtypeSt...  54.9 us
    transpose x1, local copies, waits for them, and re-layouts, shards(): x = jnp.transpose(spectra, (2, 1, 0, 3)).reshape(2, rows, F)  2.44 us
    reshape x1, local copies, waits for them, and re-layouts, shards(): return out.reshape(steps, bl, lag_dev)  1.49 us
    squeeze x1, local copies, waits for them, and re-layouts, shards(): slots = jnp.transpose(bin_rows[:, 0], (0, 2, 1))  1.29 us

profile of v5, /device:TPU:0, one launch (start us, length us, event | category | flops | bytes accessed | tf_op | source)
XLA Modules:
  0.0 60.2 jit_solution(11350387108548281038)
XLA Ops:
  0.0 1.3 %copy.12 = s32[4,1,32,3]{2,3,0,1:T(4,128)} copy(s32[4,1,32,3]{2,1,3,0:T(1,128)} %param.7) | data formatting | bytes 3072 | tf_op jit(solution)/shard_map/squeeze | solution.py:455
  1.3 2.4 %copy.7 = bf16[2,4,48,1024]{3,2,1,0:T(8,128)(2,1)} copy(bf16[2,4,48,1024]{3,0,1,2:T(2,128)(2,1)} %bitcast.9) | data formatting | bytes 1572864 | tf_op jit(solution)/shard_map/transpose | solution.py:446
  3.7 54.9 %stack.1 = f32[16,1024]{1,0:T(8,128)} custom-call(bf16[2,192,1024]{2,1,0:T(8,128)(2,1)} %bitcast.8, s32[4]{0:T(128)} %sources_ref.1, s32[4,3,32]{2,1,0:T(4,128)} %bitcast.10, bf16[4,256,256]{2,1,0:T(8,128)(2,1)} %constant.4.clone.edge_ref, bf16[8,1,4,256,256]{4,3,2,1,0:T(8,128)(2,1)} %constant.5.clone.tab_hbm), custom_call_target="tpu_custom_call" | custom-call | tf_op jit(solution)/shard_map/stack/pallas_call | solution.py:456
  58.7 1.5 %reshape.7 = f32[4,4,1024]{2,1,0:T(4,128)} reshape(f32[16,1024]{1,0:T(8,128)} %stack.1) | data formatting | bytes 131072 | tf_op jit(solution)/shard_map/reshape | solution.py:506

commit v6 on v5

--- a/solution.py
+++ b/solution.py
@@ -409,7 +409,7 @@
             bin_sums(v - 1, *jobs[-1])
             copy1(v - 1).start()
 
-        for stage, lag in ((stage2, 1), (stage3, 3), (stage4, 5), (stage5, 7)):
+        for stage, lag in ((stage5, 7), (stage4, 5), (stage3, 3), (stage2, 1)):
             @pl.when((v >= lag) & (v < units + lag))
             def _(stage=stage, lag=lag):
                 stage(v - lag)

time: 60.4 us -> 60.7 us (level)
  no operation moved by 1% of the time
where the time goes in v6:
time: 60.7 us; the launch traced here: 60.4 us
  Pallas kernels  55.2 us (91%)
  local copies, waits for them, and re-layouts  5.22 us (9%)
    pallas_call x1, Pallas kernels, shards(): pl.pallas_call(functools.partial(kernel, cfg), out_shape=jax.ShapeDtypeSt...  55.2 us
    transpose x1, local copies, waits for them, and re-layouts, shards(): x = jnp.transpose(spectra, (2, 1, 0, 3)).reshape(2, rows, F)  2.44 us
    reshape x1, local copies, waits for them, and re-layouts, shards(): return out.reshape(steps, bl, lag_dev)  1.49 us
    squeeze x1, local copies, waits for them, and re-layouts, shards(): slots = jnp.transpose(bin_rows[:, 0], (0, 2, 1))  1.29 us

profile of v6, /device:TPU:0, one launch (start us, length us, event | category | flops | bytes accessed | tf_op | source)
XLA Modules:
  0.0 60.4 jit_solution(9345704402757924927)
XLA Ops:
  0.0 1.3 %copy.12 = s32[4,1,32,3]{2,3,0,1:T(4,128)} copy(s32[4,1,32,3]{2,1,3,0:T(1,128)} %param.7) | data formatting | bytes 3072 | tf_op jit(solution)/shard_map/squeeze | solution.py:455
  1.3 2.4 %copy.7 = bf16[2,4,48,1024]{3,2,1,0:T(8,128)(2,1)} copy(bf16[2,4,48,1024]{3,0,1,2:T(2,128)(2,1)} %bitcast.9) | data formatting | bytes 1572864 | tf_op jit(solution)/shard_map/transpose | solution.py:446
  3.7 55.2 %stack.1 = f32[16,1024]{1,0:T(8,128)} custom-call(bf16[2,192,1024]{2,1,0:T(8,128)(2,1)} %bitcast.8, s32[4]{0:T(128)} %sources_ref.1, s32[4,3,32]{2,1,0:T(4,128)} %bitcast.10, bf16[4,256,256]{2,1,0:T(8,128)(2,1)} %constant.4.clone.edge_ref, bf16[8,1,4,256,256]{4,3,2,1,0:T(8,128)(2,1)} %constant.5.clone.tab_hbm), custom_call_target="tpu_custom_call" | custom-call | tf_op jit(solution)/shard_map/stack/pallas_call | solution.py:456
  58.9 1.5 %reshape.7 = f32[4,4,1024]{2,1,0:T(4,128)} reshape(f32[16,1024]{1,0:T(8,128)} %stack.1) | data formatting | bytes 131072 | tf_op jit(solution)/shard_map/reshape | solution.py:506
